TPU v7x, 32 devices: a whole 2x2x4 slice. The times are simulated.
32 devices in a mesh: grp: 4 (over z), cell: 8 (over y, x, core).
Axes of the slice: x: 2, y: 2, z: 4, core: 2. Of those that a mesh axis runs over, the one named last changes fastest.
Arguments:
- load: float32 [32, 2048, 256], P(('grp', 'cell')), may hold values from -6 to 6
- schur: bfloat16 [32, 2048, 2048], P(('grp', 'cell')), as said below
- local_inverse: bfloat16 [32, 2048, 2048], P(('grp', 'cell')), as said below
- face_map: int32 [32, 4, 512], P(('grp', 'cell')), may hold values from 0 to 511, as said below
- primal_basis: bfloat16 [32, 32, 2048], P(('grp', 'cell')), may hold values from -0.25 to 0.25
- primal_index: int32 [32, 32], P(('grp', 'cell')), may hold values from 0 to 255
- group_inverse: float32 [4, 256, 256], P('grp', 'cell'), as said below
- group_to_coarsest: float32 [4, 256, 128], P('grp', 'cell'), may hold values from -0.375 to 0.375
- coarsest_inverse: float32 [128, 128], replicated, as said below
Outputs:
- solution: float32 [32, 2048, 256], P(('grp', 'cell'))
- residual: float32 [32, 2048, 256], P(('grp', 'cell'))
Inputs may be any that keep to these rules, and one draw needn't show every extreme that they name: face_map[i, f] is a permutation of 0 .. 511, and the maps of two neighbouring cells across their shared face are inverse to each other. `schur`: each cell's matrix is symmetric positive definite. `local_inverse`: each cell's matrix is symmetric positive definite. `group_inverse`: each row's matrix is symmetric positive definite. `coarsest_inverse`: symmetric positive definite.
All inputs are finite; a program needn't handle non-finite values.
Results may differ from a plain program's by a relative error of at most 0.0066.
Values sent between devices are 32-bit elements; how exact they have to be, the bound alone decides.
No kernel may reach another device: no remote copies, remote signals or barrier semaphores. Data moves between devices by JAX's collectives and lax.ppermute only.
A program may use at most 128 MiB of HBM per device.

v0:
```python
import functools

import jax
import jax.numpy as jnp
from jax import lax
from jax.experimental import pallas as pl
from jax.experimental.pallas import tpu as pltpu
from jax.sharding import PartitionSpec as P

HIGHEST = lax.Precision.HIGHEST
EXTRA = 8
F32, BF16 = jnp.float32, jnp.bfloat16
ANY = pl.BlockSpec(memory_space=pl.ANY)
VMEM = pl.BlockSpec(memory_space=pltpu.VMEM)


def high_dot(a, b):
    return jnp.dot(a, b, precision=HIGHEST)


def wide(a, b):
    return jnp.dot(a, b, preferred_element_type=F32)


def pairs(count, odd):
    return [p for i in range(odd, count - 1, 2) for p in ((i, i + 1), (i + 1, i))]


def exchange(parts):
    return [
        lax.ppermute(part, axis, pairs(lax.axis_size(axis), odd))
        for part, (axis, odd) in zip(parts, (("grp", 0), ("grp", 1), ("cell", 0), ("cell", 1)))
    ]


def slots():
    faces, weights = [], []
    for axis, low in (("grp", 2), ("cell", 0)):
        index, count = lax.axis_index(axis), lax.axis_size(axis)
        odd = lax.rem(index, 2)
        for up in (1 - odd, odd):
            there = jnp.where(up == 1, index < count - 1, index > 0)
            faces.append(low + up)
            weights.append(jnp.where(there, 0.5, 1.0).astype(F32))
    return faces, weights


class Copies:
    def __init__(self, sems):
        self.sems, self.used = sems, 0

    def start(self, source, target):
        copy = pltpu.make_async_copy(source, target, self.sems.at[self.used])
        self.used += 1
        copy.start()
        return copy


def rows_of(face, size):
    return pl.ds(pl.multiple_of(face * size, size), size)


def split(values):
    high = values.astype(BF16)
    low = (values - high.astype(F32)).astype(BF16)
    return jnp.concatenate([high, low], axis=1)


def exact(matrix, values):
    both = wide(matrix, split(values))
    half = both.shape[1] // 2
    return both[:, :half] + both[:, half:]


def column_sums(values):
    return jnp.sum(values, axis=0, keepdims=True)


def call(kernel, inputs, specs, outs, out_specs, scratch, copies, flops):
    moved = sum(a.size * a.dtype.itemsize for a in inputs)
    return pl.pallas_call(
        kernel,
        out_shape=outs,
        in_specs=specs,
        out_specs=out_specs,
        scratch_shapes=[*scratch, pltpu.SemaphoreType.DMA((copies,))],
        compiler_params=pltpu.CompilerParams(vmem_limit_bytes=40 * 2**20),
        cost_estimate=pl.CostEstimate(flops=flops, bytes_accessed=moved, transcendentals=0),
    )(*inputs)


def split_faces(load):
    size, columns = load.shape[0] // 4, load.shape[1]

    def kernel(load_ref, *refs):
        outs, sems = refs[:4], refs[4]
        faces, _ = slots()
        moves = Copies(sems)
        for copy in [moves.start(load_ref.at[rows_of(faces[s], size)], outs[s]) for s in range(4)]:
            copy.wait()

    return call(
        kernel,
        [load],
        [ANY],
        [jax.ShapeDtypeStruct((size, columns), F32)] * 4,
        [ANY] * 4,
        [],
        4,
        0,
    )


def gather_primal(own, got, orders, basis, sums):
    size, columns = own[0].shape
    prim = basis.shape[0]
    whole = (4 * size, columns)

    def kernel(*refs):
        own_refs, got_refs, (order_ref, basis_ref, sums_ref) = refs[:4], refs[4:8], refs[8:11]
        full_ref, half_ref, sent_ref = refs[11:14]
        own_buf, got_buf, order_buf, full_buf, half_buf, sems = refs[14:]
        faces, weights = slots()
        moves = Copies(sems)
        loads = [
            (
                moves.start(got_refs[s], got_buf.at[s]),
                moves.start(order_ref.at[faces[s]], order_buf.at[s]),
                moves.start(own_refs[s], own_buf.at[s]),
            )
            for s in range(4)
        ]
        stores = []
        for s in range(4):
            for copy in loads[s]:
                copy.wait()
            full = own_buf[s] + exact(order_buf[s], got_buf[s])
            rows = rows_of(faces[s], size)
            full_buf[s] = full
            stores.append(moves.start(full_buf.at[s], full_ref.at[rows]))
            half_buf[rows, :] = (full * weights[s]).astype(BF16)
        stores.append(moves.start(half_buf, half_ref))
        sent_ref[:prim, :] = wide(basis_ref[...], half_buf[...])
        sent_ref[prim:, :] = sums_ref[...]
        for copy in stores:
            copy.wait()

    return call(
        kernel,
        [*own, *got, orders, basis, sums],
        [ANY] * 9 + [VMEM] * 2,
        [
            jax.ShapeDtypeStruct(whole, F32),
            jax.ShapeDtypeStruct(whole, BF16),
            jax.ShapeDtypeStruct((prim + EXTRA, columns), F32),
        ],
        [ANY, ANY, VMEM],
        [
            pltpu.VMEM((4, size, columns), F32),
            pltpu.VMEM((4, size, columns), F32),
            pltpu.VMEM((4, size, size), BF16),
            pltpu.VMEM((4, size, columns), F32),
            pltpu.VMEM(whole, BF16),
        ],
        17,
        2 * 4 * size * columns * (2 * size + prim),
    )


def solve_first(half, matrix, lift, picked):
    n, columns = half.shape
    size = n // 4

    def kernel(half_ref, matrix_ref, lift_ref, picked_ref, *refs):
        outs, (half_buf, matrix_buf, out_buf, sems) = refs[:4], refs[4:]
        faces, weights = slots()
        moves = Copies(sems)
        first = moves.start(half_ref, half_buf)
        loads = [
            moves.start(matrix_ref.at[rows_of(faces[s], size)], matrix_buf.at[s]) for s in range(4)
        ]
        picked = split(picked_ref[...])
        first.wait()
        stores = []
        for s in range(4):
            raised = wide(lift_ref[rows_of(faces[s], size), :], picked)
            raised = raised[:, :columns] + raised[:, columns:]
            loads[s].wait()
            out_buf[s] = (wide(matrix_buf[s], half_buf[...]) + raised) * weights[s]
            stores.append(moves.start(out_buf.at[s], outs[s]))
        for copy in stores:
            copy.wait()

    return call(
        kernel,
        [half, matrix, lift, picked],
        [ANY, ANY, VMEM, VMEM],
        [jax.ShapeDtypeStruct((size, columns), F32)] * 4,
        [ANY] * 4,
        [
            pltpu.VMEM((n, columns), BF16),
            pltpu.VMEM((4, size, n), BF16),
            pltpu.VMEM((4, size, columns), F32),
        ],
        9,
        2 * n * columns * n,
    )


def solve_second(residual, image, matrix, lift, picked, sent):
    n, columns = residual.shape
    size = n // 4
    prim = picked.shape[0]

    def kernel(residual_ref, image_ref, matrix_ref, lift_ref, picked_ref, sent_ref, *refs):
        outs, next_ref, total_ref = refs[:4], refs[4], refs[5]
        res_buf, image_buf, half_buf, matrix_buf, out_buf, sems = refs[6:]
        faces, weights = slots()
        moves = Copies(sems)
        early = []
        for s in range(4):
            rows = rows_of(faces[s], size)
            early.append(
                (
                    moves.start(residual_ref.at[rows], res_buf.at[s]),
                    moves.start(image_ref.at[rows], image_buf.at[s]),
                )
            )
        loads = [
            moves.start(matrix_ref.at[rows_of(faces[s], size)], matrix_buf.at[s]) for s in range(4)
        ]
        total = jnp.sum(sent_ref[...], axis=0)
        total_ref[...] = total[prim:]
        alpha = total[prim : prim + 1] / total[prim + 1 : prim + 2]
        picked = split(picked_ref[...] - alpha * total[:prim])
        stores = []
        for s in range(4):
            for copy in early[s]:
                copy.wait()
            rows = rows_of(faces[s], size)
            res = res_buf[s] - alpha * image_buf[s]
            res_buf[s] = res
            stores.append(moves.start(res_buf.at[s], next_ref.at[rows]))
            half_buf[rows, :] = (res * weights[s]).astype(BF16)
        for s in range(4):
            raised = wide(lift_ref[rows_of(faces[s], size), :], picked)
            raised = raised[:, :columns] + raised[:, columns:]
            loads[s].wait()
            out_buf[s] = (wide(matrix_buf[s], half_buf[...]) + raised) * weights[s]
            stores.append(moves.start(out_buf.at[s], outs[s]))
        for copy in stores:
            copy.wait()

    return call(
        kernel,
        [residual, image, matrix, lift, picked, sent],
        [ANY, ANY, ANY, VMEM, VMEM, VMEM],
        [jax.ShapeDtypeStruct((size, columns), F32)] * 4
        + [
            jax.ShapeDtypeStruct((n, columns), F32),
            jax.ShapeDtypeStruct((sent.shape[1] - prim, columns), F32),
        ],
        [ANY] * 5 + [VMEM],
        [
            pltpu.VMEM((4, size, columns), F32),
            pltpu.VMEM((4, size, columns), F32),
            pltpu.VMEM((n, columns), BF16),
            pltpu.VMEM((4, size, n), BF16),
            pltpu.VMEM((4, size, columns), F32),
        ],
        20,
        2 * n * columns * n,
    )


def image_of(own, got, orders, matrix, residual, past):
    size, columns = own[0].shape
    n = 4 * size
    extra = len(past)

    def kernel(*refs):
        own_refs, got_refs, (order_ref, matrix_ref, residual_ref) = refs[:4], refs[4:8], refs[8:11]
        past_refs, refs = refs[11 : 11 + extra], refs[11 + extra :]
        search_ref, outs, sums_ref = refs[0], refs[1:5], refs[5]
        own_buf, got_buf, order_buf, res_buf, half_buf, matrix_buf, out_buf, past_buf, sems = refs[6:]
        faces, weights = slots()
        moves = Copies(sems)
        early = [
            (
                moves.start(got_refs[s], got_buf.at[s]),
                moves.start(order_ref.at[faces[s]], order_buf.at[s]),
                moves.start(own_refs[s], own_buf.at[s]),
            )
            for s in range(4)
        ]
        late = []
        for s in range(4):
            rows = rows_of(faces[s], size)
            late.append([moves.start(matrix_ref.at[rows], matrix_buf.at[s])])
        for s in range(4):
            late[s].append(moves.start(residual_ref.at[rows_of(faces[s], size)], res_buf.at[s]))
            if extra:
                late[s].append(moves.start(past_refs[s], past_buf.at[s]))
        stores = []
        for s in range(4):
            for copy in early[s]:
                copy.wait()
            search = own_buf[s] + exact(order_buf[s], got_buf[s])
            rows = rows_of(faces[s], size)
            own_buf[s] = search
            stores.append(moves.start(own_buf.at[s], search_ref.at[rows]))
            half_buf[rows, :] = search.astype(BF16)
        sums = [jnp.zeros((1, columns), F32) for _ in range(3)]
        for s in range(4):
            for copy in late[s]:
                copy.wait()
            image = wide(matrix_buf[s], half_buf[...])
            out_buf[s] = image
            stores.append(moves.start(out_buf.at[s], outs[s]))
            search = own_buf[s]
            sums[0] += weights[s] * column_sums(res_buf[s] * search)
            sums[1] += column_sums(search * image)
            if extra:
                sums[2] += column_sums(search * past_buf[s])
        sums_ref[...] = jnp.concatenate(sums + [jnp.zeros((EXTRA - 3, columns), F32)], axis=0)
        for copy in stores:
            copy.wait()

    return call(
        kernel,
        [*own, *got, orders, matrix, residual, *past],
        [ANY] * (11 + extra),
        [jax.ShapeDtypeStruct((n, columns), F32)]
        + [jax.ShapeDtypeStruct((size, columns), F32)] * 4
        + [jax.ShapeDtypeStruct((EXTRA, columns), F32)],
        [ANY] * 5 + [VMEM],
        [
            pltpu.VMEM((4, size, columns), F32),
            pltpu.VMEM((4, size, columns), F32),
            pltpu.VMEM((4, size, size), BF16),
            pltpu.VMEM((4, size, columns), F32),
            pltpu.VMEM((n, columns), BF16),
            pltpu.VMEM((4, size, n), BF16),
            pltpu.VMEM((4, size, columns), F32),
            pltpu.VMEM((4, size, columns) if extra else (1, 8, 128), F32),
        ],
        32,
        2 * n * columns * (n + 2 * size),
    )


def finish(own, got, orders, search, second, residual, image, total, sums):
    size, columns = own[0].shape
    n = 4 * size

    def kernel(*refs):
        own_refs, got_refs, order_ref = refs[:4], refs[4:8], refs[8]
        whole_refs, (total_ref, sums_ref) = refs[9:13], refs[13:15]
        out_refs = refs[15:17]
        own_buf, got_buf, order_buf, whole_buf, sems = refs[17:]
        faces, _ = slots()
        moves = Copies(sems)
        loads = []
        for s in range(4):
            rows = rows_of(faces[s], size)
            loads.append(
                [
                    moves.start(got_refs[s], got_buf.at[s]),
                    moves.start(order_ref.at[faces[s]], order_buf.at[s]),
                    moves.start(own_refs[s], own_buf.at[s]),
                ]
                + [moves.start(whole_refs[k].at[rows], whole_buf.at[k, s]) for k in range(4)]
            )
        product, curvature = total_ref[0:1, :], total_ref[1:2, :]
        sums = jnp.sum(sums_ref[...], axis=0)
        alpha = product / curvature
        beta = sums[0:1] / product
        alpha_next = sums[0:1] / (sums[1:2] + beta * (2.0 * sums[2:3] + beta * curvature))
        stores = []
        for s in range(4):
            for copy in loads[s]:
                copy.wait()
            rows = rows_of(faces[s], size)
            image = own_buf[s] + exact(order_buf[s], got_buf[s]) + beta * whole_buf[3, s]
            own_buf[s] = whole_buf[2, s] - alpha_next * image
            search = whole_buf[0, s]
            got_buf[s] = alpha * search + alpha_next * (whole_buf[1, s] + beta * search)
            stores.append(moves.start(got_buf.at[s], out_refs[0].at[rows]))
            stores.append(moves.start(own_buf.at[s], out_refs[1].at[rows]))
        for copy in stores:
            copy.wait()

    return call(
        kernel,
        [*own, *got, orders, search, second, residual, image, total, sums],
        [ANY] * 13 + [VMEM] * 2,
        [jax.ShapeDtypeStruct((n, columns), F32)] * 2,
        [ANY] * 2,
        [
            pltpu.VMEM((4, size, columns), F32),
            pltpu.VMEM((4, size, columns), F32),
            pltpu.VMEM((4, size, size), BF16),
            pltpu.VMEM((4, 4, size, columns), F32),
        ],
        36,
        2 * n * columns * 2 * size,
    )


def body(
    load,
    schur,
    local_inverse,
    face_map,
    primal_basis,
    primal_index,
    group_inverse,
    group_to_coarsest,
    coarsest_inverse,
):
    groups = lax.axis_size("grp")
    cells = lax.axis_size("cell")
    grp_index = lax.axis_index("grp")
    ifaces, columns = load.shape[1:]
    prim = primal_basis.shape[1]
    owned, row_unknowns = group_inverse.shape[1:]
    coarsest_n = coarsest_inverse.shape[0]
    schur, local_inverse, basis = schur[0], local_inverse[0], primal_basis[0]
    face = ifaces // 4
    block = prim + EXTRA

    own = split_faces(load[0])
    got = exchange(own)
    orders = (face_map[0][:, :, None] == lax.iota(jnp.int32, face)[None, None, :]).astype(BF16)
    lift = basis.T

    width = row_unknowns + coarsest_n
    index_row = jnp.pad(primal_index.astype(F32), ((0, 7), (0, width - prim)))
    level = jnp.concatenate(
        [jnp.concatenate([group_inverse[0], group_to_coarsest[0]], axis=1), index_row], axis=0
    )
    level = lax.all_gather(level, "cell", axis=0, tiled=False)
    row_inverse = level[:, :owned, :row_unknowns].reshape(row_unknowns, row_unknowns)
    lifting = level[:, :owned, row_unknowns:].reshape(row_unknowns, coarsest_n)
    row_index = level[:, owned, :prim]
    row_index = jnp.pad(row_index, ((0, 0), (0, EXTRA)), constant_values=-1.0)
    row_index = row_index.reshape(1, cells * block)
    spread = (row_index == lax.iota(F32, row_unknowns)[:, None]).astype(F32)
    picks = (primal_index[0][:, None] == lax.iota(jnp.int32, row_unknowns)[None, :]).astype(F32)
    own_map = high_dot(high_dot(picks, row_inverse), spread)
    down_map = high_dot(lifting.T, spread)
    up_map = high_dot(high_dot(picks, lifting), coarsest_inverse)

    residual, half, sent = gather_primal(own, got, orders, basis, jnp.zeros((EXTRA, columns), F32))
    row_primal = lax.all_gather(sent, "cell", axis=0, tiled=True)
    sent = jnp.concatenate([high_dot(down_map, row_primal), up_map.reshape(-1, columns)])
    sent = lax.all_gather(sent, "grp", axis=0, tiled=False)
    coarsest = jnp.sum(sent[:, :coarsest_n], axis=0)
    up_all = sent[:, coarsest_n:].reshape(groups * prim, coarsest_n)
    picked = high_dot(own_map, row_primal) + high_dot(up_map, coarsest)

    mine = (lax.iota(jnp.int32, groups) == grp_index).astype(F32)[:, None, None]
    chain = high_dot(up_all, down_map).reshape(groups, prim, cells * block) + mine * own_map[None]
    sums_map = jnp.tile(jnp.eye(EXTRA, block, prim, dtype=F32), (1, cells))
    chain = jnp.concatenate(
        [chain, jnp.broadcast_to(sums_map[None], (groups,) + sums_map.shape)], axis=1
    ).reshape(groups * block, cells * block)

    own = solve_first(half, local_inverse, lift, picked)
    search, *own, sums = image_of(own, exchange(own), orders, schur, residual, ())
    image, _, sent = gather_primal(own, exchange(own), orders, basis, sums)
    sent = lax.all_gather(sent, "cell", axis=0, tiled=True)
    sent = lax.all_to_all(high_dot(chain, sent), "grp", 0, 0, tiled=True)
    *shared, residual, total = solve_second(
        residual, image, local_inverse, lift, picked, sent.reshape(groups, block, columns)
    )
    second, *own, sums = image_of(shared, exchange(shared), orders, schur, residual, own)
    sums = jnp.broadcast_to(sums[None], (groups * cells, EXTRA, columns))
    got = exchange(own)
    sums = lax.all_to_all(sums, ("grp", "cell"), 0, 0, tiled=True)
    result, residual = finish(own, got, orders, search, second, residual, image, total, sums)
    return result[None], residual[None]


def solution(mesh):
    split_axes = ("grp", "cell")
    placed = (
        P(split_axes, None, None),
        P(split_axes, None, None),
        P(split_axes, None, None),
        P(split_axes, None, None),
        P(split_axes, None, None),
        P(split_axes, None),
        P("grp", "cell", None),
        P("grp", "cell", None),
        P(),
    )
    return jax.shard_map(
        body,
        mesh=mesh,
        in_specs=placed,
        out_specs=(P(split_axes, None, None), P(split_axes, None, None)),
        check_vma=False,
    )
```

profile of v0, /device:TPU:0, one launch (start us, length us, event | category | flops | bytes accessed | tf_op | source)
XLA Modules:
  0.0 220.4 jit_solution(10328832812785991417)
XLA Ops:
  0.7 1.6 copy-done.10
  2.3 1.2 shard_map.104
  3.5 3.1 %collective-permute-start = (f32[512,256]{1,0:T(8,128)S(1)}, f32[512,256]{1,0:T(8,128)}, u32[]{:S(2)}, u32[]{:S(2)}) collective-permute-start(f32[512,256]{1,0:T(8,128)S(1)} %get-tuple-element.35.refs_0_), channel_id=1, source_target_pairs={{0,8},{8,0},{16,24},{24,16},{1,9},{9,1},{17,25},{25,17},{2,10},{10... | collective-permute-start | bytes 1572872 | tf_op jit(solution)/shard_map/ppermute | solution.py:31
  6.6 1.5 collective-permute-start.1
  8.1 1.5 collective-permute-start.3
  9.6 18.3 %all-gather = f32[320,384]{1,0:T(8,128)S(1)} all-gather(f32[40,384]{1,0:T(8,128)S(1)} %select_maximum_fusion), channel_id=2, replica_groups=mesh['grp'=4,'cell'=8] {'cell'}, dimensions={0}, use_global_device_ids=true | all-gather | bytes 552960 | tf_op jit(solution)/shard_map/all_gather | solution.py:442
  29.0 0.6 reshape.56
  29.9 0.5 fusion.1
  30.4 1.2 fusion.refs_8_
  31.6 4.7 %shard_map.105 = (f32[2048,256]{1,0:T(8,128)S(1)}, bf16[2048,256]{1,0:T(8,128)(2,1)S(1)}, f32[40,256]{1,0:T(8,128)S(1)}) custom-call(f32[512,256]{1,0:T(8,128)S(1)} %get-tuple-element.35.refs_0_, f32[512,256]{1,0:T(8,128)} %get-tuple-element.36.refs_1_, f32[512,256]{1,0:T(8,128)} %get-tuple-element.37.refs_2_, f32[512,256]{1,0:T(8,128)} %get-tuple-element.38.refs_3_, ...), custom_call_target="tpu_custom_call" | custom-call | flops 1107296256 | bytes 6430720 | tf_op jit(solution)/shard_map/pallas_call | solution.py:81
  36.4 11.9 %all_gather.20 = f32[320,256]{1,0:T(8,128)S(1)} all-gather(f32[40,256]{1,0:T(8,128)S(1)} %get-tuple-element.41), channel_id=1, replica_groups=mesh['grp'=4,'cell'=8] {'cell'}, dimensions={0}, use_global_device_ids=true | all-gather | bytes 368640 | tf_op jit(solution)/shard_map/all_gather | solution.py:455
  48.3 0.5 fusion.18
  48.8 17.4 %all-gather.1 = f32[576,256]{1,0:T(8,128)S(1)} all-gather(f32[144,256]{1,0:T(8,128)S(1)} %pad_maximum_fusion), channel_id=3, replica_groups=mesh['grp'=4,'cell'=8] {'grp'}, dimensions={0}, use_global_device_ids=true | all-gather | bytes 737280 | tf_op jit(solution)/shard_map/all_gather | solution.py:457
  67.0 7.0 %shard_map.106 = (f32[512,256]{1,0:T(8,128)S(1)}, f32[512,256]{1,0:T(8,128)}, f32[512,256]{1,0:T(8,128)}, f32[512,256]{1,0:T(8,128)}) custom-call(bf16[2048,256]{1,0:T(8,128)(2,1)S(1)} %get-tuple-element.40.half_ref, bf16[2048,2048]{1,0:T(8,128)(2,1)S(1)} %bitcast.39, bf16[2048,32]{1,0:T(8,128)(2,1)S(1)} %bitcast.40, ...), custom_call_target="tpu_custom_call" | custom-call | flops 2147483648 | bytes 9601024 | tf_op jit(solution)/shard_map/pallas_call | solution.py:81
  74.0 1.1 collective-permute-start.4
  75.2 0.8 copy-done.12
  76.0 1.5 collective-permute-start.5
  77.4 1.5 collective-permute-start.7
  78.9 7.9 %collective-permute-done.4.refs_4_ = f32[512,256]{1,0:T(8,128)} collective-permute-done((f32[512,256]{1,0:T(8,128)S(1)}, f32[512,256]{1,0:T(8,128)}, u32[]{:S(2)}, u32[]{:S(2)}) %collective-permute-start.4) | collective-permute-done | bytes 524320 | tf_op jit(solution)/shard_map/ppermute | solution.py:31
  86.8 1.6 copy-done.6
  88.4 1.0 copy-done.13
  89.4 10.2 %shard_map.107 = (f32[2048,256]{1,0:T(8,128)S(1)}, f32[512,256]{1,0:T(8,128)S(1)}, f32[512,256]{1,0:T(8,128)}, f32[512,256]{1,0:T(8,128)}, f32[512,256]{1,0:T(8,128)}, /*index=5*/f32[8,256]{1,0:T(8,128)S(1)}) custom-call(f32[512,256]{1,0:T(8,128)S(1)} %copy-done.13, f32[512,256]{1,0:T(8,128)} %get-tuple-element.43.refs_1_, ...), custom_call_target="tpu_custom_call" | custom-call | flops 3221225472 | bytes 16777216 | tf_op jit(solution)/shard_map/pallas_call | solution.py:81
  99.7 1.3 copy-done.8
  101.0 4.6 %collective-permute-start.8 = (f32[512,256]{1,0:T(8,128)S(1)}, f32[512,256]{1,0:T(8,128)}, u32[]{:S(2)}, u32[]{:S(2)}) collective-permute-start(f32[512,256]{1,0:T(8,128)S(1)} %get-tuple-element.46.refs_0_.refs_11_), channel_id=1, source_target_pairs={{0,8},{8,0},{16,24},{24,16},{1,9},{9,1},{17,25},{25,17},{2,10},{10... | collective-permute-start | bytes 1572872 | tf_op jit(solution)/shard_map/ppermute | solution.py:31
  105.6 1.5 collective-permute-start.9
  107.1 5.4 %collective-permute-start.10 = (f32[512,256]{1,0:T(8,128)}, f32[512,256]{1,0:T(8,128)}, u32[]{:S(2)}, u32[]{:S(2)}) collective-permute-start(f32[512,256]{1,0:T(8,128)} %get-tuple-element.48.refs_2_.refs_13_), channel_id=1, source_target_pairs={{0,1},{1,0},{2,3},{3,2},{4,5},{5,4},{6,7},{7,6},{8,9},{9,8},{10,11... | collective-permute-start | bytes 1572872 | tf_op jit(solution)/shard_map/ppermute | solution.py:31
  112.4 1.5 collective-permute-start.11
  114.0 0.6 tile.8
  114.6 1.4 tile.9
  116.0 1.5 slice.24
  117.5 1.5 dot_general.40
  119.0 1.2 convolution_add_fusion
  120.2 5.3 %shard_map.108 = (f32[2048,256]{1,0:T(8,128)S(1)}, bf16[2048,256]{1,0:T(8,128)(2,1)}, f32[40,256]{1,0:T(8,128)S(1)}) custom-call(f32[512,256]{1,0:T(8,128)S(1)} %get-tuple-element.46.refs_0_.refs_11_, f32[512,256]{1,0:T(8,128)} %get-tuple-element.47.refs_1_.refs_12_, f32[512,256]{1,0:T(8,128)} %get-tuple-element.48.refs_2_.refs_13_, ...), custom_call_target="tpu_custom_call" | custom-call | flops 1107296256 | bytes 6430720 | tf_op jit(solution)/shard_map/pallas_call | solution.py:81
  125.6 18.3 %all_gather.23 = f32[320,256]{1,0:T(8,128)S(1)} all-gather(f32[40,256]{1,0:T(8,128)S(1)} %get-tuple-element.52), channel_id=1, replica_groups=mesh['grp'=4,'cell'=8] {'cell'}, dimensions={0}, use_global_device_ids=true | all-gather | bytes 368640 | tf_op jit(solution)/shard_map/all_gather | solution.py:472
  144.3 10.3 %all_to_all.11.sent_ref = f32[4,40,256]{2,1,0:T(8,128)S(1)} all-to-all(f32[4,40,256]{2,1,0:T(8,128)S(1)} %fusion.3), channel_id=1, replica_groups=mesh['grp'=4,'cell'=8] {'grp'}, dimensions={0} | all-to-all | bytes 327680 | tf_op jit(solution)/shard_map/all_to_all | solution.py:473
  154.6 8.0 %shard_map.109 = (f32[512,256]{1,0:T(8,128)S(1)}, f32[512,256]{1,0:T(8,128)S(1)}, f32[512,256]{1,0:T(8,128)S(1)}, f32[512,256]{1,0:T(8,128)S(1)}, f32[2048,256]{1,0:T(8,128)S(1)}, /*index=5*/f32[8,256]{1,0:T(8,128)S(1)}) custom-call(f32[2048,256]{1,0:T(8,128)S(1)} %copy-done.7, f32[2048,256]{1,0:T(8,128)S(1)} %get-tuple-element.51.image_ref.refs_12_, ...), custom_call_target="tpu_custom_call" | custom-call | flops 2147483648 | bytes 12910592 | tf_op jit(solution)/shard_map/pallas_call | solution.py:81
  162.6 1.3 copy-done.3
  163.9 0.7 collective-permute-start.12
  164.5 0.7 collective-permute-start.13
  165.3 0.7 collective-permute-start.15
  166.0 10.7 %collective-permute-done.12.refs_4_ = f32[512,256]{1,0:T(8,128)S(1)} collective-permute-done((f32[512,256]{1,0:T(8,128)S(1)}, f32[512,256]{1,0:T(8,128)S(1)}, u32[]{:S(2)}, u32[]{:S(2)}) %collective-permute-start.12) | collective-permute-done | bytes 524320 | tf_op jit(solution)/shard_map/ppermute | solution.py:31
  176.7 10.2 %shard_map.110 = (f32[2048,256]{1,0:T(8,128)S(1)}, f32[512,256]{1,0:T(8,128)S(1)}, f32[512,256]{1,0:T(8,128)S(1)}, f32[512,256]{1,0:T(8,128)S(1)}, f32[512,256]{1,0:T(8,128)S(1)}, /*index=5*/f32[8,256]{1,0:T(8,128)S(1)}) custom-call(f32[512,256]{1,0:T(8,128)S(1)} %get-tuple-element.53.refs_0_, f32[512,256]{1,0:T(8,128)S(1)} %get-tuple-element.54.refs_1_, ...), custom_call_target="tpu_custom_call" | custom-call | flops 3221225472 | bytes 18874368 | tf_op jit(solution)/shard_map/pallas_call | solution.py:81
  186.9 3.7 %collective-permute-start.16 = (f32[512,256]{1,0:T(8,128)S(1)}, f32[512,256]{1,0:T(8,128)S(1)}, u32[]{:S(2)}, u32[]{:S(2)}) collective-permute-start(f32[512,256]{1,0:T(8,128)S(1)} %get-tuple-element.58.refs_0_), channel_id=1, source_target_pairs={{0,8},{8,0},{16,24},{24,16},{1,9},{9,1},{17,25},{25,17},{2,10},{10... | collective-permute-start | bytes 1572872 | tf_op jit(solution)/shard_map/ppermute | solution.py:31
  190.6 0.7 collective-permute-start.17
  191.3 3.3 %collective-permute-start.18 = (f32[512,256]{1,0:T(8,128)S(1)}, f32[512,256]{1,0:T(8,128)S(1)}, u32[]{:S(2)}, u32[]{:S(2)}) collective-permute-start(f32[512,256]{1,0:T(8,128)S(1)} %get-tuple-element.60.refs_2_), channel_id=1, source_target_pairs={{0,1},{1,0},{2,3},{3,2},{4,5},{5,4},{6,7},{7,6},{8,9},{9,8},{10,11... | collective-permute-start | bytes 1572872 | tf_op jit(solution)/shard_map/ppermute | solution.py:31
  194.6 0.7 collective-permute-start.19
  195.4 19.5 %all_to_all.12.refs_14_ = f32[32,8,256]{2,1,0:T(8,128)S(1)} all-to-all(f32[32,8,256]{2,1,0:T(8,128)S(1)} %broadcast_in_dim.12), channel_id=1, replica_groups=mesh['grp'=4,'cell'=8] {'grp','cell'}, dimensions={0} | all-to-all | bytes 524288 | tf_op jit(solution)/shard_map/all_to_all | solution.py:480
  214.9 5.3 %shard_map.111 = (f32[2048,256]{1,0:T(8,128)}, f32[2048,256]{1,0:T(8,128)}) custom-call(f32[512,256]{1,0:T(8,128)S(1)} %get-tuple-element.58.refs_0_, f32[512,256]{1,0:T(8,128)S(1)} %get-tuple-element.59.refs_1_, f32[512,256]{1,0:T(8,128)S(1)} %get-tuple-element.60.refs_2_, f32[512,256]{1,0:T(8,128)S(1)} %get-tuple-element.61.refs_3_, ...), custom_call_target="tpu_custom_call" | custom-call | flops 1073741824 | bytes 14950400 | tf_op jit(solution)/shard_map/pallas_call | solution.py:81
  (84 shorter events, 2.8 us)
Async XLA Ops:
  0.6 27.9 %copy-start = (f32[128,128]{1,0:T(8,128)S(1)}, f32[128,128]{1,0:T(8,128)}, u32[]{:S(2)}) copy-start(f32[128,128]{1,0:T(8,128)} %param.17) | copy-start | bytes 196612
  0.6 8.9 %copy-start.22 = (s32[1,32]{1,0:T(1,128)S(1)}, s32[1,32]{1,0:T(1,128)}, u32[]{:S(2)}) copy-start(s32[1,32]{1,0:T(1,128)} %param.14) | copy-start | bytes 388
  0.7 1.6 copy-start.10
  2.3 7.3 %copy-start.20 = (f32[1,32,256]{2,1,0:T(8,128)S(1)}, f32[1,32,256]{2,1,0:T(8,128)}, u32[]{:S(2)}) copy-start(f32[1,32,256]{2,1,0:T(8,128)} %param.15) | copy-start | bytes 98308
  2.3 7.3 %copy-start.21 = (f32[1,32,128]{2,1,0:T(8,128)S(1)}, f32[1,32,128]{2,1,0:T(8,128)}, u32[]{:S(2)}) copy-start(f32[1,32,128]{2,1,0:T(8,128)} %param.16) | copy-start | bytes 49156
  2.3 27.3 %copy-start.11 = (bf16[1,32,2048]{2,1,0:T(8,128)(2,1)S(1)}, bf16[1,32,2048]{2,1,0:T(8,128)(2,1)}, u32[]{:S(2)}) copy-start(bf16[1,32,2048]{2,1,0:T(8,128)(2,1)} %param.13) | copy-start | bytes 393220
  3.5 28.1 %collective-permute-start = (f32[512,256]{1,0:T(8,128)S(1)}, f32[512,256]{1,0:T(8,128)}, u32[]{:S(2)}, u32[]{:S(2)}) collective-permute-start(f32[512,256]{1,0:T(8,128)S(1)} %get-tuple-element.35.refs_0_), channel_id=1, source_target_pairs={{0,8},{8,0},{16,24},{24,16},{1,9},{9,1},{17,25},{25,17},{2,10},{10... | collective-permute-start | bytes 1572872 | tf_op jit(solution)/shard_map/ppermute | solution.py:31
  6.6 25.0 %collective-permute-start.1 = (f32[512,256]{1,0:T(8,128)}, f32[512,256]{1,0:T(8,128)}, u32[]{:S(2)}, u32[]{:S(2)}) collective-permute-start(f32[512,256]{1,0:T(8,128)} %get-tuple-element.36.refs_1_), channel_id=1, source_target_pairs={{8,16},{16,8},{9,17},{17,9},{10,18},{18,10},{11,19},{19,11},{12,20... | collective-permute-start | bytes 1572872 | tf_op jit(solution)/shard_map/ppermute | solution.py:31
  8.1 23.5 %collective-permute-start.2 = (f32[512,256]{1,0:T(8,128)}, f32[512,256]{1,0:T(8,128)}, u32[]{:S(2)}, u32[]{:S(2)}) collective-permute-start(f32[512,256]{1,0:T(8,128)} %get-tuple-element.37.refs_2_), channel_id=1, source_target_pairs={{0,1},{1,0},{2,3},{3,2},{4,5},{5,4},{6,7},{7,6},{8,9},{9,8},{10,11... | collective-permute-start | bytes 1572872 | tf_op jit(solution)/shard_map/ppermute | solution.py:31
  8.1 23.5 %collective-permute-start.3 = (f32[512,256]{1,0:T(8,128)}, f32[512,256]{1,0:T(8,128)}, u32[]{:S(2)}, u32[]{:S(2)}) collective-permute-start(f32[512,256]{1,0:T(8,128)} %get-tuple-element.38.refs_3_), channel_id=1, source_target_pairs={{1,2},{2,1},{3,4},{4,3},{5,6},{6,5},{9,10},{10,9},{11,12},{12,11},... | collective-permute-start | bytes 1572872 | tf_op jit(solution)/shard_map/ppermute | solution.py:31
  28.7 0.9 copy-start.16
  29.0 37.5 %copy-start.15 = (f32[32,320]{1,0:T(8,128)}, f32[32,320]{1,0:T(8,128)S(1)}, u32[]{:S(2)}) copy-start(f32[32,320]{1,0:T(8,128)S(1)} %fusion.2) | copy-start | bytes 122884
  30.4 18.4 %copy-start.18 = (f32[16,256]{1,0:T(8,128)S(1)}, f32[16,256]{1,0:T(8,128)}, u32[]{:S(2)}) copy-start(f32[16,256]{1,0:T(8,128)} %reshape.56) | copy-start | bytes 49156
  31.6 35.4 %copy-start.1 = (bf16[1,2048,2048]{2,1,0:T(8,128)(2,1)S(1)}, bf16[1,2048,2048]{2,1,0:T(8,128)(2,1)}, u32[]{:S(2)}) copy-start(bf16[1,2048,2048]{2,1,0:T(8,128)(2,1)} %param.11) | copy-start | bytes 25165828
  36.4 37.6 %copy-start.5 = (f32[2048,256]{1,0:T(8,128)}, f32[2048,256]{1,0:T(8,128)S(1)}, u32[]{:S(2)}) copy-start(f32[2048,256]{1,0:T(8,128)S(1)} %get-tuple-element.39.refs_10_.residual_ref) | copy-start | bytes 6291460
  36.4 29.8 %copy-start.17 = (f32[32,128]{1,0:T(8,128)S(1)}, f32[32,128]{1,0:T(8,128)}, u32[]{:S(2)}) copy-start(f32[32,128]{1,0:T(8,128)} %copy-done.16) | copy-start | bytes 49156
  66.2 0.8 copy-start.14
  74.0 12.8 %collective-permute-start.4 = (f32[512,256]{1,0:T(8,128)S(1)}, f32[512,256]{1,0:T(8,128)}, u32[]{:S(2)}, u32[]{:S(2)}) collective-permute-start(f32[512,256]{1,0:T(8,128)S(1)} %get-tuple-element.42.refs_0_), channel_id=1, source_target_pairs={{0,8},{8,0},{16,24},{24,16},{1,9},{9,1},{17,25},{25,17},{2,10},{10... | collective-permute-start | bytes 1572872 | tf_op jit(solution)/shard_map/ppermute | solution.py:31
  75.2 0.8 copy-start.12
  76.0 10.8 %collective-permute-start.5 = (f32[512,256]{1,0:T(8,128)}, f32[512,256]{1,0:T(8,128)}, u32[]{:S(2)}, u32[]{:S(2)}) collective-permute-start(f32[512,256]{1,0:T(8,128)} %get-tuple-element.43.refs_1_), channel_id=1, source_target_pairs={{8,16},{16,8},{9,17},{17,9},{10,18},{18,10},{11,19},{19,11},{12,20... | collective-permute-start | bytes 1572872 | tf_op jit(solution)/shard_map/ppermute | solution.py:31
  77.4 9.4 %collective-permute-start.6 = (f32[512,256]{1,0:T(8,128)}, f32[512,256]{1,0:T(8,128)}, u32[]{:S(2)}, u32[]{:S(2)}) collective-permute-start(f32[512,256]{1,0:T(8,128)} %get-tuple-element.44.refs_2_), channel_id=1, source_target_pairs={{0,1},{1,0},{2,3},{3,2},{4,5},{5,4},{6,7},{7,6},{8,9},{9,8},{10,11... | collective-permute-start | bytes 1572872 | tf_op jit(solution)/shard_map/ppermute | solution.py:31
  77.4 9.4 %collective-permute-start.7 = (f32[512,256]{1,0:T(8,128)}, f32[512,256]{1,0:T(8,128)}, u32[]{:S(2)}, u32[]{:S(2)}) collective-permute-start(f32[512,256]{1,0:T(8,128)} %get-tuple-element.45.refs_3_), channel_id=1, source_target_pairs={{1,2},{2,1},{3,4},{4,3},{5,6},{6,5},{9,10},{10,9},{11,12},{12,11},... | collective-permute-start | bytes 1572872 | tf_op jit(solution)/shard_map/ppermute | solution.py:31
  86.8 1.6 copy-start.6
  88.4 1.0 copy-start.13
  99.7 1.3 copy-start.8
  101.0 19.2 %collective-permute-start.8 = (f32[512,256]{1,0:T(8,128)S(1)}, f32[512,256]{1,0:T(8,128)}, u32[]{:S(2)}, u32[]{:S(2)}) collective-permute-start(f32[512,256]{1,0:T(8,128)S(1)} %get-tuple-element.46.refs_0_.refs_11_), channel_id=1, source_target_pairs={{0,8},{8,0},{16,24},{24,16},{1,9},{9,1},{17,25},{25,17},{2,10},{10... | collective-permute-start | bytes 1572872 | tf_op jit(solution)/shard_map/ppermute | solution.py:31
  105.6 14.5 %collective-permute-start.9 = (f32[512,256]{1,0:T(8,128)}, f32[512,256]{1,0:T(8,128)}, u32[]{:S(2)}, u32[]{:S(2)}) collective-permute-start(f32[512,256]{1,0:T(8,128)} %get-tuple-element.47.refs_1_.refs_12_), channel_id=1, source_target_pairs={{8,16},{16,8},{9,17},{17,9},{10,18},{18,10},{11,19},{19,11},{12,20... | collective-permute-start | bytes 1572872 | tf_op jit(solution)/shard_map/ppermute | solution.py:31
  107.1 13.1 %collective-permute-start.10 = (f32[512,256]{1,0:T(8,128)}, f32[512,256]{1,0:T(8,128)}, u32[]{:S(2)}, u32[]{:S(2)}) collective-permute-start(f32[512,256]{1,0:T(8,128)} %get-tuple-element.48.refs_2_.refs_13_), channel_id=1, source_target_pairs={{0,1},{1,0},{2,3},{3,2},{4,5},{5,4},{6,7},{7,6},{8,9},{9,8},{10,11... | collective-permute-start | bytes 1572872 | tf_op jit(solution)/shard_map/ppermute | solution.py:31
  112.4 7.7 %collective-permute-start.11 = (f32[512,256]{1,0:T(8,128)}, f32[512,256]{1,0:T(8,128)}, u32[]{:S(2)}, u32[]{:S(2)}) collective-permute-start(f32[512,256]{1,0:T(8,128)} %get-tuple-element.49.refs_3_.refs_14_), channel_id=1, source_target_pairs={{1,2},{2,1},{3,4},{4,3},{5,6},{6,5},{9,10},{10,9},{11,12},{12,11},... | collective-permute-start | bytes 1572872 | tf_op jit(solution)/shard_map/ppermute | solution.py:31
  120.2 23.7 %copy-start.19 = (f32[8,320]{1,0:T(8,128)S(1)}, f32[8,320]{1,0:T(8,128)}, u32[]{:S(2)}) copy-start(f32[8,320]{1,0:T(8,128)} %tile.9) | copy-start | bytes 30724
  120.2 34.4 %copy-start.7 = (f32[2048,256]{1,0:T(8,128)S(1)}, f32[2048,256]{1,0:T(8,128)}, u32[]{:S(2)}) copy-start(f32[2048,256]{1,0:T(8,128)} %copy-done.5) | copy-start | bytes 6291460
  125.6 37.0 %copy-start.2 = (f32[2048,256]{1,0:T(8,128)}, f32[2048,256]{1,0:T(8,128)S(1)}, u32[]{:S(2)}) copy-start(f32[2048,256]{1,0:T(8,128)S(1)} %get-tuple-element.51.image_ref.refs_12_) | copy-start | bytes 6291460
  162.6 1.3 copy-start.3
  163.9 12.8 %collective-permute-start.12 = (f32[512,256]{1,0:T(8,128)S(1)}, f32[512,256]{1,0:T(8,128)S(1)}, u32[]{:S(2)}, u32[]{:S(2)}) collective-permute-start(f32[512,256]{1,0:T(8,128)S(1)} %get-tuple-element.53.refs_0_), channel_id=1, source_target_pairs={{0,8},{8,0},{16,24},{24,16},{1,9},{9,1},{17,25},{25,17},{2,10},{10... | collective-permute-start | bytes 1572872 | tf_op jit(solution)/shard_map/ppermute | solution.py:31
  164.5 12.1 %collective-permute-start.13 = (f32[512,256]{1,0:T(8,128)S(1)}, f32[512,256]{1,0:T(8,128)S(1)}, u32[]{:S(2)}, u32[]{:S(2)}) collective-permute-start(f32[512,256]{1,0:T(8,128)S(1)} %get-tuple-element.54.refs_1_), channel_id=1, source_target_pairs={{8,16},{16,8},{9,17},{17,9},{10,18},{18,10},{11,19},{19,11},{12,20... | collective-permute-start | bytes 1572872 | tf_op jit(solution)/shard_map/ppermute | solution.py:31
  165.2 11.5 %collective-permute-start.14 = (f32[512,256]{1,0:T(8,128)S(1)}, f32[512,256]{1,0:T(8,128)S(1)}, u32[]{:S(2)}, u32[]{:S(2)}) collective-permute-start(f32[512,256]{1,0:T(8,128)S(1)} %get-tuple-element.55.refs_2_), channel_id=1, source_target_pairs={{0,1},{1,0},{2,3},{3,2},{4,5},{5,4},{6,7},{7,6},{8,9},{9,8},{10,11... | collective-permute-start | bytes 1572872 | tf_op jit(solution)/shard_map/ppermute | solution.py:31
  165.3 11.4 %collective-permute-start.15 = (f32[512,256]{1,0:T(8,128)S(1)}, f32[512,256]{1,0:T(8,128)S(1)}, u32[]{:S(2)}, u32[]{:S(2)}) collective-permute-start(f32[512,256]{1,0:T(8,128)S(1)} %get-tuple-element.56.refs_3_), channel_id=1, source_target_pairs={{1,2},{2,1},{3,4},{4,3},{5,6},{6,5},{9,10},{10,9},{11,12},{12,11},... | collective-permute-start | bytes 1572872 | tf_op jit(solution)/shard_map/ppermute | solution.py:31
  176.7 38.2 %copy-start.4 = (f32[2048,256]{1,0:T(8,128)S(1)}, f32[2048,256]{1,0:T(8,128)}, u32[]{:S(2)}) copy-start(f32[2048,256]{1,0:T(8,128)} %copy-done.3) | copy-start | bytes 6291460
  176.7 38.1 %copy-start.9 = (f32[2048,256]{1,0:T(8,128)S(1)}, f32[2048,256]{1,0:T(8,128)}, u32[]{:S(2)}) copy-start(f32[2048,256]{1,0:T(8,128)} %copy-done.8) | copy-start | bytes 6291460
  186.9 27.9 %collective-permute-start.16 = (f32[512,256]{1,0:T(8,128)S(1)}, f32[512,256]{1,0:T(8,128)S(1)}, u32[]{:S(2)}, u32[]{:S(2)}) collective-permute-start(f32[512,256]{1,0:T(8,128)S(1)} %get-tuple-element.58.refs_0_), channel_id=1, source_target_pairs={{0,8},{8,0},{16,24},{24,16},{1,9},{9,1},{17,25},{25,17},{2,10},{10... | collective-permute-start | bytes 1572872 | tf_op jit(solution)/shard_map/ppermute | solution.py:31
  190.6 24.2 %collective-permute-start.17 = (f32[512,256]{1,0:T(8,128)S(1)}, f32[512,256]{1,0:T(8,128)S(1)}, u32[]{:S(2)}, u32[]{:S(2)}) collective-permute-start(f32[512,256]{1,0:T(8,128)S(1)} %get-tuple-element.59.refs_1_), channel_id=1, source_target_pairs={{8,16},{16,8},{9,17},{17,9},{10,18},{18,10},{11,19},{19,11},{12,20... | collective-permute-start | bytes 1572872 | tf_op jit(solution)/shard_map/ppermute | solution.py:31
  191.3 23.5 %collective-permute-start.18 = (f32[512,256]{1,0:T(8,128)S(1)}, f32[512,256]{1,0:T(8,128)S(1)}, u32[]{:S(2)}, u32[]{:S(2)}) collective-permute-start(f32[512,256]{1,0:T(8,128)S(1)} %get-tuple-element.60.refs_2_), channel_id=1, source_target_pairs={{0,1},{1,0},{2,3},{3,2},{4,5},{5,4},{6,7},{7,6},{8,9},{9,8},{10,11... | collective-permute-start | bytes 1572872 | tf_op jit(solution)/shard_map/ppermute | solution.py:31
  194.6 20.2 %collective-permute-start.19 = (f32[512,256]{1,0:T(8,128)S(1)}, f32[512,256]{1,0:T(8,128)S(1)}, u32[]{:S(2)}, u32[]{:S(2)}) collective-permute-start(f32[512,256]{1,0:T(8,128)S(1)} %get-tuple-element.61.refs_3_), channel_id=1, source_target_pairs={{1,2},{2,1},{3,4},{4,3},{5,6},{6,5},{9,10},{10,9},{11,12},{12,11},... | collective-permute-start | bytes 1572872 | tf_op jit(solution)/shard_map/ppermute | solution.py:31
where the time goes:
time: 221 us; the launch traced here: 220 us
  blocking collectives  95.6 us (43%)
  Pallas kernels  52 us (24%)
  starting transfers between devices  33.5 us (15%)
  waiting for transfers between devices  18.6 us (8%)
  local copies, waits for them, and re-layouts  14.1 us (6%)
  matrix products  3.88 us (2%)
    pallas_call x8, Pallas kernels, call(): pl.pallas_call(kernel, out_shape=outs, in_specs=specs, out_specs=out_spec...  52 us
    ppermute x20, starting transfers between devices, exchange(): lax.ppermute(part, axis, pairs(lax.axis_size(axis), odd))  33.5 us
    all_to_all x1, blocking collectives, body(): sums = lax.all_to_all(sums, ('grp', 'cell'), 0, 0, tiled=True)  19.5 us
    ppermute x20, waiting for transfers between devices, exchange(): lax.ppermute(part, axis, pairs(lax.axis_size(axis), odd))  18.6 us
    all_gather x1, blocking collectives, body(): level = lax.all_gather(level, 'cell', axis=0, tiled=False)  18.3 us
    all_gather x1, blocking collectives, body(): sent = lax.all_gather(sent, 'cell', axis=0, tiled=True)  18.3 us
    all_gather x1, blocking collectives, body(): sent = lax.all_gather(sent, 'grp', axis=0, tiled=False)  17.4 us
    all_gather x1, blocking collectives, body(): row_primal = lax.all_gather(sent, 'cell', axis=0, tiled=True)  11.9 us
  transfers between devices with their start and end apart: 20, of which 2 were waited for; matrix products, arithmetic and copies ran while one was open for 4% of the time, Pallas kernels for 0%

commit v1 on v0

v1 whole, which is shorter than its diff:
```python
import functools

import jax
import jax.numpy as jnp
from jax import lax
from jax.experimental import pallas as pl
from jax.experimental.pallas import tpu as pltpu
from jax.sharding import PartitionSpec as P

HIGHEST = lax.Precision.HIGHEST
EXTRA = 8
F32, BF16 = jnp.float32, jnp.bfloat16
ANY = pl.BlockSpec(memory_space=pl.ANY)
VMEM = pl.BlockSpec(memory_space=pltpu.VMEM)


def high_dot(a, b):
    return jnp.dot(a, b, precision=HIGHEST)


def wide(a, b):
    return jnp.dot(a, b, preferred_element_type=F32)


def pairs(count, odd):
    return [p for i in range(odd, count - 1, 2) for p in ((i, i + 1), (i + 1, i))]


def exchange(parts):
    return [
        lax.ppermute(part, axis, pairs(lax.axis_size(axis), odd))
        for part, (axis, odd) in zip(parts, (("grp", 0), ("grp", 1), ("cell", 0), ("cell", 1)))
    ]


def slots():
    faces, weights = [], []
    for axis, low in (("grp", 2), ("cell", 0)):
        index, count = lax.axis_index(axis), lax.axis_size(axis)
        odd = lax.rem(index, 2)
        for up in (1 - odd, odd):
            there = jnp.where(up == 1, index < count - 1, index > 0)
            faces.append(low + up)
            weights.append(jnp.where(there, 0.5, 1.0).astype(F32))
    return faces, weights


def rows_of(face, size):
    return pl.ds(pl.multiple_of(face * size, size), size)


def split(values):
    high = values.astype(BF16)
    low = (values - high.astype(F32)).astype(BF16)
    return jnp.concatenate([high, low], axis=1)


def exact(matrix, values):
    both = wide(matrix, split(values))
    half = both.shape[1] // 2
    return both[:, :half] + both[:, half:]


def column_sums(values):
    return jnp.sum(values, axis=0, keepdims=True)


def stacked(values, pieces):
    width = values.shape[1] // pieces
    return jnp.concatenate([values[:, k * width : (k + 1) * width] for k in range(pieces)], axis=0)


def beside(values, pieces):
    height = values.shape[0] // pieces
    return jnp.concatenate(
        [values[k * height : (k + 1) * height] for k in range(pieces)], axis=1
    )


def call(kernel, inputs, specs, outs, out_specs, scratch, flops):
    moved = sum(a.size * a.dtype.itemsize for a in inputs)
    return pl.pallas_call(
        kernel,
        out_shape=outs,
        in_specs=specs,
        out_specs=out_specs,
        scratch_shapes=scratch,
        compiler_params=pltpu.CompilerParams(vmem_limit_bytes=24 * 2**20),
        cost_estimate=pl.CostEstimate(flops=flops, bytes_accessed=moved // 8, transcendentals=0),
    )(*inputs)


def shape(*dims):
    return jax.ShapeDtypeStruct(dims, F32)


def split_faces(load):
    size, columns = load.shape[0] // 4, load.shape[1]

    def kernel(load_ref, *refs):
        outs, sems = refs[:4], refs[4]
        faces, _ = slots()
        copies = [
            pltpu.make_async_copy(load_ref.at[rows_of(faces[s], size)], outs[s], sems.at[s])
            for s in range(4)
        ]
        for copy in copies:
            copy.start()
        for copy in copies:
            copy.wait()

    return call(
        kernel,
        [load],
        [ANY],
        [shape(size, columns)] * 4,
        [VMEM] * 4,
        [pltpu.SemaphoreType.DMA((4,))],
        0,
    )


def gather_primal(own, got, orders, basis, tail):
    size, columns = own[0].shape
    prim = basis.shape[0]
    whole = (4 * size, columns)

    def kernel(*refs):
        own_refs, got_refs, (order_ref, basis_ref, tail_ref) = refs[:4], refs[4:8], refs[8:11]
        full_ref, half_ref, sent_ref = refs[11:]
        faces, weights = slots()
        sent_ref[prim:, :] = tail_ref[...]
        for s in range(4):
            full = own_refs[s][...] + exact(order_ref[faces[s]], got_refs[s][...])
            full_ref[s] = full
            half_ref[rows_of(faces[s], size), :] = (full * weights[s]).astype(BF16)
        sent_ref[:prim, :] = wide(basis_ref[...], half_ref[...])

    return call(
        kernel,
        [*own, *got, orders, basis, tail],
        [VMEM] * 11,
        [
            shape(4, size, columns),
            jax.ShapeDtypeStruct(whole, BF16),
            shape(prim + tail.shape[0], columns),
        ],
        [VMEM] * 3,
        [],
        2 * 4 * size * columns * (2 * size + prim),
    )


class Level:
    def __init__(self, prim, owned, unknowns, coarsest, columns):
        self.prim, self.owned, self.unknowns, self.coarsest = prim, owned, unknowns, coarsest
        self.inverse_pieces, self.lift_pieces = unknowns // columns, columns // coarsest
        self.at_inverse = prim
        self.at_lift = self.at_inverse + owned * self.inverse_pieces
        self.at_index = self.at_lift + owned // self.lift_pieces
        self.columns = columns

    def tail(self, inverse, lift, index):
        index = jnp.pad(index.astype(F32), ((0, 7), (0, self.columns - self.prim)))
        return jnp.concatenate(
            [stacked(inverse, self.inverse_pieces), beside(lift, self.lift_pieces), index], axis=0
        )

    def read(self, ref, cells):
        inverse, lift, index = [], [], []
        for cell in range(cells):
            inverse.append(beside(ref[cell, self.at_inverse : self.at_lift, :], self.inverse_pieces))
            lift.append(stacked(ref[cell, self.at_lift : self.at_index, :], self.lift_pieces))
            index.append(ref[cell, self.at_index : self.at_index + 1, : self.prim])
        inverse, lift = jnp.concatenate(inverse, axis=0), jnp.concatenate(lift, axis=0)
        index = jnp.concatenate(index, axis=1).astype(jnp.int32)
        rows = lax.broadcasted_iota(jnp.int32, (self.unknowns, cells * self.prim), 0)
        return inverse, lift, (rows == index).astype(F32)

    def primal(self, ref, cells):
        return jnp.concatenate([ref[cell, : self.prim, :] for cell in range(cells)], axis=0)

    def picks(self, ref):
        columns = lax.broadcasted_iota(jnp.int32, (self.prim, self.unknowns), 1)
        return (columns == ref[...]).astype(F32)


def lower_first(level, gathered, index, coarsest_inverse):
    cells, _, columns = gathered.shape

    def kernel(gathered_ref, index_ref, coarsest_ref, sent_ref, own_ref, up_ref):
        inverse, lift, spread = level.read(gathered_ref, cells)
        picks = level.picks(index_ref)
        coarse = high_dot(spread, level.primal(gathered_ref, cells))
        own_ref[...] = high_dot(high_dot(picks, inverse), coarse)
        up = high_dot(high_dot(picks, lift), coarsest_ref[...])
        up_ref[...] = up
        sent_ref[: level.coarsest, :] = high_dot(lift.T, coarse)
        sent_ref[level.coarsest :, :] = beside(up, level.lift_pieces)

    return call(
        kernel,
        [gathered, index, coarsest_inverse],
        [VMEM] * 3,
        [
            shape(level.coarsest + level.prim // level.lift_pieces, columns),
            shape(level.prim, columns),
            shape(level.prim, level.coarsest),
        ],
        [VMEM] * 3,
        [],
        0,
    )


def lower_second(level, gathered, index, ups, again):
    cells, block, columns = again.shape
    groups = ups.shape[0]

    def kernel(gathered_ref, index_ref, ups_ref, again_ref, sent_ref):
        inverse, lift, spread = level.read(gathered_ref, cells)
        picks = level.picks(index_ref)
        coarse = high_dot(spread, level.primal(again_ref, cells))
        own = high_dot(high_dot(picks, inverse), coarse)
        lowered = high_dot(lift.T, coarse)
        sums = again_ref[0, level.prim :, :]
        for cell in range(1, cells):
            sums = sums + again_ref[cell, level.prim :, :]
        mine = lax.axis_index("grp")
        for row in range(groups):
            up = stacked(ups_ref[row, level.coarsest :, :], level.lift_pieces)
            sent_ref[row, : level.prim, :] = high_dot(up, lowered) + jnp.where(
                mine == row, own, jnp.zeros_like(own)
            )
            sent_ref[row, level.prim :, :] = sums

    return call(
        kernel,
        [gathered, index, ups, again],
        [VMEM] * 4,
        shape(groups, block, columns),
        VMEM,
        [],
        0,
    )


def solve_first(half, matrix, lift, own, up, sent):
    n, columns = half.shape
    size = n // 4
    prim, coarsest_n = up.shape

    def kernel(half_ref, matrix_ref, lift_ref, own_ref, up_ref, sent_ref, *refs):
        outs, picked_ref = refs[:4], refs[4]
        faces, weights = slots()
        coarsest = jnp.sum(sent_ref[:, :coarsest_n, :], axis=0)
        picked = own_ref[...] + high_dot(up_ref[...], coarsest)
        picked_ref[...] = picked
        picked = split(picked)
        for s in range(4):
            rows = rows_of(faces[s], size)
            raised = wide(lift_ref[rows, :], picked)
            raised = raised[:, :columns] + raised[:, columns:]
            outs[s][...] = (wide(matrix_ref[rows, :], half_ref[...]) + raised) * weights[s]

    return call(
        kernel,
        [half, matrix, lift, own, up, sent],
        [VMEM] * 6,
        [shape(size, columns)] * 4 + [shape(prim, columns)],
        [VMEM] * 5,
        [],
        2 * n * columns * n,
    )


def solve_second(residual, image, matrix, lift, picked, sent):
    _, size, columns = residual.shape
    n = 4 * size
    prim = picked.shape[0]

    def kernel(residual_ref, image_ref, matrix_ref, lift_ref, picked_ref, sent_ref, *refs):
        outs, next_ref, total_ref, half_ref = refs[:4], refs[4], refs[5], refs[6]
        faces, weights = slots()
        total = jnp.sum(sent_ref[...], axis=0)
        total_ref[...] = total[prim:]
        alpha = total[prim : prim + 1] / total[prim + 1 : prim + 2]
        picked = split(picked_ref[...] - alpha * total[:prim])
        for s in range(4):
            res = residual_ref[s] - alpha * image_ref[s]
            next_ref[s] = res
            half_ref[rows_of(faces[s], size), :] = (res * weights[s]).astype(BF16)
        for s in range(4):
            rows = rows_of(faces[s], size)
            raised = wide(lift_ref[rows, :], picked)
            raised = raised[:, :columns] + raised[:, columns:]
            outs[s][...] = (wide(matrix_ref[rows, :], half_ref[...]) + raised) * weights[s]

    return call(
        kernel,
        [residual, image, matrix, lift, picked, sent],
        [VMEM] * 6,
        [shape(size, columns)] * 4
        + [shape(4, size, columns), shape(sent.shape[1] - prim, columns)],
        [VMEM] * 6,
        [pltpu.VMEM((n, columns), BF16)],
        2 * n * columns * n,
    )


def image_of(own, got, orders, matrix, residual, past):
    size, columns = own[0].shape
    n = 4 * size
    extra = len(past)

    def kernel(*refs):
        own_refs, got_refs, (order_ref, matrix_ref, residual_ref) = refs[:4], refs[4:8], refs[8:11]
        past_refs, refs = refs[11 : 11 + extra], refs[11 + extra :]
        search_ref, outs, sums_ref, half_ref = refs[0], refs[1:5], refs[5], refs[6]
        faces, weights = slots()
        for s in range(4):
            search = own_refs[s][...] + exact(order_ref[faces[s]], got_refs[s][...])
            search_ref[s] = search
            half_ref[rows_of(faces[s], size), :] = search.astype(BF16)
        sums = [jnp.zeros((1, columns), F32) for _ in range(3)]
        for s in range(4):
            image = wide(matrix_ref[rows_of(faces[s], size), :], half_ref[...])
            outs[s][...] = image
            search = search_ref[s]
            sums[0] += weights[s] * column_sums(residual_ref[s] * search)
            sums[1] += column_sums(search * image)
            if extra:
                sums[2] += column_sums(search * past_refs[s][...])
        sums_ref[...] = jnp.concatenate(sums + [jnp.zeros((EXTRA - 3, columns), F32)], axis=0)

    return call(
        kernel,
        [*own, *got, orders, matrix, residual, *past],
        [VMEM] * (11 + extra),
        [shape(4, size, columns)] + [shape(size, columns)] * 4 + [shape(EXTRA, columns)],
        [VMEM] * 6,
        [pltpu.VMEM((n, columns), BF16)],
        2 * n * columns * (n + 2 * size),
    )


def finish(own, got, orders, search, second, residual, image, total, sums):
    size, columns = own[0].shape
    n = 4 * size

    def kernel(*refs):
        own_refs, got_refs, order_ref = refs[:4], refs[4:8], refs[8]
        search_ref, second_ref, residual_ref, image_ref, total_ref, sums_ref = refs[9:15]
        out_refs, (solution_buf, residual_buf, sems) = refs[15:17], refs[17:]
        faces, _ = slots()
        product, curvature = total_ref[0:1, :], total_ref[1:2, :]
        sums = jnp.sum(sums_ref[...], axis=0)
        alpha = product / curvature
        beta = sums[0:1] / product
        alpha_next = sums[0:1] / (sums[1:2] + beta * (2.0 * sums[2:3] + beta * curvature))
        stores = []
        for s in range(4):
            rows = rows_of(faces[s], size)
            image = own_refs[s][...] + exact(order_ref[faces[s]], got_refs[s][...])
            residual_buf[s] = residual_ref[s] - alpha_next * (image + beta * image_ref[s])
            search = search_ref[s]
            solution_buf[s] = alpha * search + alpha_next * (second_ref[s] + beta * search)
            for k, buf in enumerate((solution_buf, residual_buf)):
                copy = pltpu.make_async_copy(buf.at[s], out_refs[k].at[rows], sems.at[2 * s + k])
                copy.start()
                stores.append(copy)
        for copy in stores:
            copy.wait()

    return call(
        kernel,
        [*own, *got, orders, search, second, residual, image, total, sums],
        [VMEM] * 15,
        [shape(n, columns)] * 2,
        [ANY] * 2,
        [
            pltpu.VMEM((4, size, columns), F32),
            pltpu.VMEM((4, size, columns), F32),
            pltpu.SemaphoreType.DMA((8,)),
        ],
        2 * n * columns * 2 * size,
    )


def body(
    load,
    schur,
    local_inverse,
    face_map,
    primal_basis,
    primal_index,
    group_inverse,
    group_to_coarsest,
    coarsest_inverse,
):
    groups = lax.axis_size("grp")
    cells = lax.axis_size("cell")
    ifaces, columns = load.shape[1:]
    prim = primal_basis.shape[1]
    owned, row_unknowns = group_inverse.shape[1:]
    coarsest_n = coarsest_inverse.shape[0]
    schur, local_inverse, basis = schur[0], local_inverse[0], primal_basis[0]
    face = ifaces // 4
    level = Level(prim, owned, row_unknowns, coarsest_n, columns)

    own = split_faces(load[0])
    got = exchange(own)
    orders = (face_map[0][:, :, None] == lax.iota(jnp.int32, face)[None, None, :]).astype(BF16)
    lift = basis.T
    index = primal_index.reshape(prim, 1)
    tail = level.tail(group_inverse[0], group_to_coarsest[0], primal_index)

    residual, half, sent = gather_primal(own, got, orders, basis, tail)
    gathered = lax.all_gather(sent, "cell", axis=0, tiled=False)
    sent, picked, up = lower_first(level, gathered, index, coarsest_inverse)
    ups = lax.all_gather(sent, "grp", axis=0, tiled=False)
    *own, picked = solve_first(half, local_inverse, lift, picked, up, ups)
    search, *own, sums = image_of(own, exchange(own), orders, schur, residual, ())
    image, _, sent = gather_primal(own, exchange(own), orders, basis, sums)
    again = lax.all_gather(sent, "cell", axis=0, tiled=False)
    sent = lower_second(level, gathered, index, ups, again)
    sent = lax.all_to_all(sent, "grp", 0, 0, tiled=True)
    *shared, residual, total = solve_second(residual, image, local_inverse, lift, picked, sent)
    second, *own, sums = image_of(shared, exchange(shared), orders, schur, residual, own)
    sums = jnp.broadcast_to(sums[None], (groups * cells, EXTRA, columns))
    got = exchange(own)
    sums = lax.all_to_all(sums, ("grp", "cell"), 0, 0, tiled=True)
    result, residual = finish(own, got, orders, search, second, residual, image, total, sums)
    return result[None], residual[None]


def solution(mesh):
    split_axes = ("grp", "cell")
    placed = (
        P(split_axes, None, None),
        P(split_axes, None, None),
        P(split_axes, None, None),
        P(split_axes, None, None),
        P(split_axes, None, None),
        P(split_axes, None),
        P("grp", "cell", None),
        P("grp", "cell", None),
        P(),
    )
    return jax.shard_map(
        body,
        mesh=mesh,
        in_specs=placed,
        out_specs=(P(split_axes, None, None), P(split_axes, None, None)),
        check_vma=False,
    )
```

time: 221 us -> 181 us (0.82)
  Pallas kernels: 52 us -> 25.3 us
  waiting for transfers between devices: 18.6 us -> 29.8 us
  local copies, waits for them, and re-layouts: 14.1 us -> 5.39 us
  blocking collectives: 95.6 us -> 88.8 us
  starting transfers between devices: 33.5 us -> 29.6 us
  matrix products: 3.88 us -> 0 us
    pallas_call x8 -> x10, Pallas kernels: 52 us -> 25.3 us  [call(): pl.pallas_call(kernel, out_shape=outs, in_specs=specs, out_specs=out_spec...]
    ppermute x20, waiting for transfers between devices: 18.6 us -> 29.8 us  [exchange(): lax.ppermute(part, axis, pairs(lax.axis_size(axis), odd))]
    all_gather x4 -> x3, blocking collectives: 65.9 us -> 58.3 us  [the longest x1 24.3 us: body(): again = lax.all_gather(sent, 'cell', axis=0, tiled=False)]
    dot_general x10 -> x0, matrix products: 3.88 us -> none  [high_dot(): return jnp.dot(a, b, precision=HIGHEST)]
    ppermute x20, starting transfers between devices: 33.5 us -> 29.6 us  [exchange(): lax.ppermute(part, axis, pairs(lax.axis_size(axis), odd))]
    unnamed x47 -> x23, local copies, waits for them, and re-layouts: 8.31 us -> 5.28 us
  transfers between devices with their start and end apart: 20 -> 20, of which waited for: 2 -> 4; matrix products, arithmetic and copies ran while one was open for 4% -> 1% of each run, Pallas kernels for 0% -> 0%
where the time goes in v1:
time: 181 us
  blocking collectives  88.8 us (49%)
  waiting for transfers between devices  29.8 us (16%)
  starting transfers between devices  29.6 us (16%)
  Pallas kernels  25.3 us (14%)
  local copies, waits for them, and re-layouts  5.39 us (3%)
    ppermute x20, waiting for transfers between devices, exchange(): lax.ppermute(part, axis, pairs(lax.axis_size(axis), odd))  29.8 us
    ppermute x20, starting transfers between devices, exchange(): lax.ppermute(part, axis, pairs(lax.axis_size(axis), odd))  29.6 us
    pallas_call x10, Pallas kernels, call(): pl.pallas_call(kernel, out_shape=outs, in_specs=specs, out_specs=out_spec...  25.3 us
    all_gather x1, blocking collectives, body(): again = lax.all_gather(sent, 'cell', axis=0, tiled=False)  24.3 us
    all_to_all x1, blocking collectives, body(): sums = lax.all_to_all(sums, ('grp', 'cell'), 0, 0, tiled=True)  19.5 us
    all_gather x1, blocking collectives, body(): ups = lax.all_gather(sent, 'grp', axis=0, tiled=False)  17.4 us
    all_gather x1, blocking collectives, body(): gathered = lax.all_gather(sent, 'cell', axis=0, tiled=False)  16.6 us
    all_to_all x1, blocking collectives, body(): sent = lax.all_to_all(sent, 'grp', 0, 0, tiled=True)  11 us
  transfers between devices with their start and end apart: 20, of which 4 were waited for; matrix products, arithmetic and copies ran while one was open for 1% of the time, Pallas kernels for 0%

profile of v1, /device:TPU:0, one launch (start us, length us, event | category | flops | bytes accessed | tf_op | source)
XLA Modules:
  0.0 180.5 jit_solution(15727264660691361420)
XLA Ops:
  0.7 1.6 copy-done.2
  2.3 0.2 shard_map.104
  2.5 3.1 %collective-permute-start = (f32[512,256]{1,0:T(8,128)S(1)}, f32[512,256]{1,0:T(8,128)S(1)}, u32[]{:S(2)}, u32[]{:S(2)}) collective-permute-start(f32[512,256]{1,0:T(8,128)S(1)} %get-tuple-element.39.refs_0_), channel_id=1, source_target_pairs={{0,8},{8,0},{16,24},{24,16},{1,9},{9,1},{17,25},{25,17},{2,10},{10... | collective-permute-start | bytes 1572872 | tf_op jit(solution)/shard_map/ppermute | solution.py:31
  5.6 1.4 collective-permute-start.1
  7.0 0.0 collective-permute-start.2
  7.0 1.5 collective-permute-start.3
  8.5 0.1 copy.13.index_ref
  8.5 0.3 copy.11
  8.9 0.0 copy-start.4
  8.9 0.5 fusion.refs_8_
  9.4 8.1 %collective-permute-done.refs_4_ = f32[512,256]{1,0:T(8,128)S(1)} collective-permute-done((f32[512,256]{1,0:T(8,128)S(1)}, f32[512,256]{1,0:T(8,128)S(1)}, u32[]{:S(2)}, u32[]{:S(2)}) %collective-permute-start) | collective-permute-done | bytes 524320 | tf_op jit(solution)/shard_map/ppermute | solution.py:31
  17.5 0.0 collective-permute-done.1.refs_5_
  17.5 0.0 copy-start
  17.5 3.3 %shard_map.105 = (f32[4,512,256]{2,1,0:T(8,128)S(1)}, bf16[2048,256]{1,0:T(8,128)(2,1)S(1)}, f32[88,256]{1,0:T(8,128)S(1)}) custom-call(f32[512,256]{1,0:T(8,128)S(1)} %get-tuple-element.39.refs_0_, f32[512,256]{1,0:T(8,128)S(1)} %get-tuple-element.40.refs_1_, f32[512,256]{1,0:T(8,128)S(1)} %get-tuple-element.41.refs_2_, ...), custom_call_target="tpu_custom_call" | custom-call | flops 1107296256 | bytes 809984 | tf_op jit(solution)/shard_map/pallas_call | solution.py:82
  20.8 16.6 %all-gather = f32[704,256]{1,0:T(8,128)S(1)} all-gather(f32[88,256]{1,0:T(8,128)S(1)} %get-tuple-element.45), channel_id=2, replica_groups=mesh['grp'=4,'cell'=8] {'cell'}, dimensions={0}, use_global_device_ids=true | all-gather | bytes 811008 | tf_op jit(solution)/shard_map/all_gather | solution.py:419
  37.4 1.1 shard_map.106
  38.5 17.4 %all-gather.1 = f32[576,256]{1,0:T(8,128)S(1)} all-gather(f32[144,256]{1,0:T(8,128)S(1)} %get-tuple-element.48), channel_id=3, replica_groups=mesh['grp'=4,'cell'=8] {'grp'}, dimensions={0}, use_global_device_ids=true | all-gather | bytes 737280 | tf_op jit(solution)/shard_map/all_gather | solution.py:421
  56.0 3.1 %shard_map.107 = (f32[512,256]{1,0:T(8,128)S(1)}, f32[512,256]{1,0:T(8,128)S(1)}, f32[512,256]{1,0:T(8,128)S(1)}, f32[512,256]{1,0:T(8,128)S(1)}, f32[32,256]{1,0:T(8,128)S(1)}) custom-call(bf16[2048,256]{1,0:T(8,128)(2,1)S(1)} %get-tuple-element.44.half_ref, bf16[2048,2048]{1,0:T(8,128)(2,1)S(1)} %bitcast.19, bf16[2048,32]{1,0:T(8,128)(2,1)S(1)} %bitcast.29, ...), custom_call_target="tpu_custom_call" | custom-call | flops 2147483648 | bytes 1275904 | tf_op jit(solution)/shard_map/pallas_call | solution.py:82
  59.1 1.1 collective-permute-start.4
  60.2 0.7 collective-permute-start.5
  60.9 0.1 collective-permute-start.6
  61.0 0.7 collective-permute-start.7
  61.7 10.1 %collective-permute-done.4.refs_4_ = f32[512,256]{1,0:T(8,128)S(1)} collective-permute-done((f32[512,256]{1,0:T(8,128)S(1)}, f32[512,256]{1,0:T(8,128)S(1)}, u32[]{:S(2)}, u32[]{:S(2)}) %collective-permute-start.4) | collective-permute-done | bytes 524320 | tf_op jit(solution)/shard_map/ppermute | solution.py:31
  71.8 0.0 copy-start.1
  71.8 3.4 %copy-done.1 = bf16[1,2048,2048]{2,1,0:T(8,128)(2,1)S(1)} copy-done((bf16[1,2048,2048]{2,1,0:T(8,128)(2,1)S(1)}, bf16[1,2048,2048]{2,1,0:T(8,128)(2,1)}, u32[]{:S(2)}) %copy-start.1) | copy-done | bytes 8388632
  75.1 3.6 %shard_map.108 = (f32[4,512,256]{2,1,0:T(8,128)S(1)}, f32[512,256]{1,0:T(8,128)S(1)}, f32[512,256]{1,0:T(8,128)S(1)}, f32[512,256]{1,0:T(8,128)S(1)}, f32[512,256]{1,0:T(8,128)S(1)}, /*index=5*/f32[8,256]{1,0:T(8,128)S(1)}) custom-call(f32[512,256]{1,0:T(8,128)S(1)} %get-tuple-element.49.refs_0_, f32[512,256]{1,0:T(8,128)S(1)} %get-tuple-element.50.refs_1_, ...), custom_call_target="tpu_custom_call" | custom-call | flops 3221225472 | bytes 2097152 | tf_op jit(solution)/shard_map/pallas_call | solution.py:82
  78.8 3.7 %collective-permute-start.8 = (f32[512,256]{1,0:T(8,128)S(1)}, f32[512,256]{1,0:T(8,128)S(1)}, u32[]{:S(2)}, u32[]{:S(2)}) collective-permute-start(f32[512,256]{1,0:T(8,128)S(1)} %get-tuple-element.53.refs_0_.refs_11_), channel_id=1, source_target_pairs={{0,8},{8,0},{16,24},{24,16},{1,9},{9,1},{17,25},{25,17},{2,10},{10... | collective-permute-start | bytes 1572872 | tf_op jit(solution)/shard_map/ppermute | solution.py:31
  82.5 0.7 collective-permute-start.9
  83.2 5.4 %collective-permute-start.10 = (f32[512,256]{1,0:T(8,128)S(1)}, f32[512,256]{1,0:T(8,128)S(1)}, u32[]{:S(2)}, u32[]{:S(2)}) collective-permute-start(f32[512,256]{1,0:T(8,128)S(1)} %get-tuple-element.55.refs_2_.refs_13_), channel_id=1, source_target_pairs={{0,1},{1,0},{2,3},{3,2},{4,5},{5,4},{6,7},{7,6},{8,9},{9,8},{10,11... | collective-permute-start | bytes 1572872 | tf_op jit(solution)/shard_map/ppermute | solution.py:31
  88.6 0.7 collective-permute-start.11
  89.3 1.0 collective-permute-done.8.refs_4_
  90.3 2.5 %shard_map.109 = (f32[4,512,256]{2,1,0:T(8,128)S(1)}, bf16[2048,256]{1,0:T(8,128)(2,1)}, f32[40,256]{1,0:T(8,128)S(1)}) custom-call(f32[512,256]{1,0:T(8,128)S(1)} %get-tuple-element.53.refs_0_.refs_11_, f32[512,256]{1,0:T(8,128)S(1)} %get-tuple-element.54.refs_1_.refs_12_, f32[512,256]{1,0:T(8,128)S(1)} %get-tuple-element.55.refs_2_.refs_13_, ...), custom_call_target="tpu_custom_call" | custom-call | flops 1107296256 | bytes 803840 | tf_op jit(solution)/shard_map/pallas_call | solution.py:82
  92.7 24.3 %all-gather.2 = f32[320,256]{1,0:T(8,128)S(1)} all-gather(f32[40,256]{1,0:T(8,128)S(1)} %get-tuple-element.60), channel_id=4, replica_groups=mesh['grp'=4,'cell'=8] {'cell'}, dimensions={0}, use_global_device_ids=true | all-gather | bytes 368640 | tf_op jit(solution)/shard_map/all_gather | solution.py:425
  117.0 1.4 shard_map.110
  118.4 11.0 %all_to_all.10.sent_ref = f32[4,40,256]{2,1,0:T(8,128)S(1)} all-to-all(f32[4,40,256]{2,1,0:T(8,128)S(1)} %shard_map.110), channel_id=1, replica_groups=mesh['grp'=4,'cell'=8] {'grp'}, dimensions={0} | all-to-all | bytes 327680 | tf_op jit(solution)/shard_map/all_to_all | solution.py:427
  129.4 2.9 %shard_map.111 = (f32[512,256]{1,0:T(8,128)S(1)}, f32[512,256]{1,0:T(8,128)S(1)}, f32[512,256]{1,0:T(8,128)S(1)}, f32[512,256]{1,0:T(8,128)S(1)}, f32[4,512,256]{2,1,0:T(8,128)S(1)}, /*index=5*/f32[8,256]{1,0:T(8,128)S(1)}) custom-call(f32[4,512,256]{2,1,0:T(8,128)S(1)} %get-tuple-element.43.refs_10_.residual_ref, ...), custom_call_target="tpu_custom_call" | custom-call | flops 2147483648 | bytes 1613824 | tf_op jit(solution)/shard_map/pallas_call | solution.py:82
  132.3 0.7 collective-permute-start.12
  133.0 0.7 collective-permute-start.13
  133.7 0.1 collective-permute-start.14
  133.8 0.7 collective-permute-start.15
  134.5 10.7 %collective-permute-done.12.refs_4_ = f32[512,256]{1,0:T(8,128)S(1)} collective-permute-done((f32[512,256]{1,0:T(8,128)S(1)}, f32[512,256]{1,0:T(8,128)S(1)}, u32[]{:S(2)}, u32[]{:S(2)}) %collective-permute-start.12) | collective-permute-done | bytes 524320 | tf_op jit(solution)/shard_map/ppermute | solution.py:31
  145.2 3.7 %shard_map.112 = (f32[4,512,256]{2,1,0:T(8,128)S(1)}, f32[512,256]{1,0:T(8,128)S(1)}, f32[512,256]{1,0:T(8,128)S(1)}, f32[512,256]{1,0:T(8,128)S(1)}, f32[512,256]{1,0:T(8,128)S(1)}, /*index=5*/f32[8,256]{1,0:T(8,128)S(1)}) custom-call(f32[512,256]{1,0:T(8,128)S(1)} %get-tuple-element.61.refs_0_, f32[512,256]{1,0:T(8,128)S(1)} %get-tuple-element.62.refs_1_, ...), custom_call_target="tpu_custom_call" | custom-call | flops 3221225472 | bytes 2359296 | tf_op jit(solution)/shard_map/pallas_call | solution.py:82
  148.9 3.7 %collective-permute-start.16 = (f32[512,256]{1,0:T(8,128)S(1)}, f32[512,256]{1,0:T(8,128)S(1)}, u32[]{:S(2)}, u32[]{:S(2)}) collective-permute-start(f32[512,256]{1,0:T(8,128)S(1)} %get-tuple-element.66.refs_0_), channel_id=1, source_target_pairs={{0,8},{8,0},{16,24},{24,16},{1,9},{9,1},{17,25},{25,17},{2,10},{10... | collective-permute-start | bytes 1572872 | tf_op jit(solution)/shard_map/ppermute | solution.py:31
  152.6 0.7 collective-permute-start.17
  153.3 3.4 %collective-permute-start.18 = (f32[512,256]{1,0:T(8,128)S(1)}, f32[512,256]{1,0:T(8,128)S(1)}, u32[]{:S(2)}, u32[]{:S(2)}) collective-permute-start(f32[512,256]{1,0:T(8,128)S(1)} %get-tuple-element.68.refs_2_), channel_id=1, source_target_pairs={{0,1},{1,0},{2,3},{3,2},{4,5},{5,4},{6,7},{7,6},{8,9},{9,8},{10,11... | collective-permute-start | bytes 1572872 | tf_op jit(solution)/shard_map/ppermute | solution.py:31
  156.7 0.7 collective-permute-start.19
  157.4 19.5 %all_to_all.11.refs_14_ = f32[32,8,256]{2,1,0:T(8,128)S(1)} all-to-all(f32[32,8,256]{2,1,0:T(8,128)S(1)} %broadcast_in_dim.6), channel_id=1, replica_groups=mesh['grp'=4,'cell'=8] {'grp','cell'}, dimensions={0} | all-to-all | bytes 524288 | tf_op jit(solution)/shard_map/all_to_all | solution.py:432
  176.9 3.4 %shard_map.113 = (f32[2048,256]{1,0:T(8,128)}, f32[2048,256]{1,0:T(8,128)}) custom-call(f32[512,256]{1,0:T(8,128)S(1)} %get-tuple-element.66.refs_0_, f32[512,256]{1,0:T(8,128)S(1)} %get-tuple-element.67.refs_1_, f32[512,256]{1,0:T(8,128)S(1)} %get-tuple-element.68.refs_2_, f32[512,256]{1,0:T(8,128)S(1)} %get-tuple-element.69.refs_3_, ...), custom_call_target="tpu_custom_call" | custom-call | flops 1073741824 | bytes 1868800 | tf_op jit(solution)/shard_map/pallas_call | solution.py:82
  (37 shorter events, 0.1 us)
Async XLA Ops:
  0.6 7.8 %copy-start.8 = (s32[1,32]{1,0:T(1,128)S(1)}, s32[1,32]{1,0:T(1,128)}, u32[]{:S(2)}) copy-start(s32[1,32]{1,0:T(1,128)} %param.14) | copy-start | bytes 388
  0.6 1.6 copy-start.2
  2.2 6.3 %copy-start.3 = (bf16[1,32,2048]{2,1,0:T(8,128)(2,1)S(1)}, bf16[1,32,2048]{2,1,0:T(8,128)(2,1)}, u32[]{:S(2)}) copy-start(bf16[1,32,2048]{2,1,0:T(8,128)(2,1)} %param.13) | copy-start | bytes 393220
  2.2 6.6 %copy-start.6 = (f32[1,32,128]{2,1,0:T(8,128)S(1)}, f32[1,32,128]{2,1,0:T(8,128)}, u32[]{:S(2)}) copy-start(f32[1,32,128]{2,1,0:T(8,128)} %param.16) | copy-start | bytes 49156
  2.2 6.6 %copy-start.5 = (f32[1,32,256]{2,1,0:T(8,128)S(1)}, f32[1,32,256]{2,1,0:T(8,128)}, u32[]{:S(2)}) copy-start(f32[1,32,256]{2,1,0:T(8,128)} %param.15) | copy-start | bytes 98308
  2.2 6.6 %copy-start.7 = (s32[1,4,512]{2,1,0:T(4,128)S(1)}, s32[1,4,512]{2,1,0:T(4,128)}, u32[]{:S(2)}) copy-start(s32[1,4,512]{2,1,0:T(4,128)} %param.12) | copy-start | bytes 24580
  2.5 15.0 %collective-permute-start = (f32[512,256]{1,0:T(8,128)S(1)}, f32[512,256]{1,0:T(8,128)S(1)}, u32[]{:S(2)}, u32[]{:S(2)}) collective-permute-start(f32[512,256]{1,0:T(8,128)S(1)} %get-tuple-element.39.refs_0_), channel_id=1, source_target_pairs={{0,8},{8,0},{16,24},{24,16},{1,9},{9,1},{17,25},{25,17},{2,10},{10... | collective-permute-start | bytes 1572872 | tf_op jit(solution)/shard_map/ppermute | solution.py:31
  5.6 11.9 %collective-permute-start.1 = (f32[512,256]{1,0:T(8,128)S(1)}, f32[512,256]{1,0:T(8,128)}, u32[]{:S(2)}, u32[]{:S(2)}) collective-permute-start(f32[512,256]{1,0:T(8,128)S(1)} %get-tuple-element.40.refs_1_), channel_id=1, source_target_pairs={{8,16},{16,8},{9,17},{17,9},{10,18},{18,10},{11,19},{19,11},{12,20... | collective-permute-start | bytes 1572872 | tf_op jit(solution)/shard_map/ppermute | solution.py:31
  7.0 10.5 %collective-permute-start.2 = (f32[512,256]{1,0:T(8,128)S(1)}, f32[512,256]{1,0:T(8,128)}, u32[]{:S(2)}, u32[]{:S(2)}) collective-permute-start(f32[512,256]{1,0:T(8,128)S(1)} %get-tuple-element.41.refs_2_), channel_id=1, source_target_pairs={{0,1},{1,0},{2,3},{3,2},{4,5},{5,4},{6,7},{7,6},{8,9},{9,8},{10,11... | collective-permute-start | bytes 1572872 | tf_op jit(solution)/shard_map/ppermute | solution.py:31
  7.0 10.5 %collective-permute-start.3 = (f32[512,256]{1,0:T(8,128)S(1)}, f32[512,256]{1,0:T(8,128)}, u32[]{:S(2)}, u32[]{:S(2)}) collective-permute-start(f32[512,256]{1,0:T(8,128)S(1)} %get-tuple-element.42.refs_3_), channel_id=1, source_target_pairs={{1,2},{2,1},{3,4},{4,3},{5,6},{6,5},{9,10},{10,9},{11,12},{12,11},... | collective-permute-start | bytes 1572872 | tf_op jit(solution)/shard_map/ppermute | solution.py:31
  8.9 28.5 %copy-start.4 = (f32[128,128]{1,0:T(8,128)S(1)}, f32[128,128]{1,0:T(8,128)}, u32[]{:S(2)}) copy-start(f32[128,128]{1,0:T(8,128)} %coarsest_ref.1) | copy-start | bytes 196612
  17.5 38.5 %copy-start = (bf16[1,2048,2048]{2,1,0:T(8,128)(2,1)S(1)}, bf16[1,2048,2048]{2,1,0:T(8,128)(2,1)}, u32[]{:S(2)}) copy-start(bf16[1,2048,2048]{2,1,0:T(8,128)(2,1)} %param.11) | copy-start | bytes 25165828
  59.1 12.7 %collective-permute-start.4 = (f32[512,256]{1,0:T(8,128)S(1)}, f32[512,256]{1,0:T(8,128)S(1)}, u32[]{:S(2)}, u32[]{:S(2)}) collective-permute-start(f32[512,256]{1,0:T(8,128)S(1)} %get-tuple-element.49.refs_0_), channel_id=1, source_target_pairs={{0,8},{8,0},{16,24},{24,16},{1,9},{9,1},{17,25},{25,17},{2,10},{10... | collective-permute-start | bytes 1572872 | tf_op jit(solution)/shard_map/ppermute | solution.py:31
  60.2 11.5 %collective-permute-start.5 = (f32[512,256]{1,0:T(8,128)S(1)}, f32[512,256]{1,0:T(8,128)S(1)}, u32[]{:S(2)}, u32[]{:S(2)}) collective-permute-start(f32[512,256]{1,0:T(8,128)S(1)} %get-tuple-element.50.refs_1_), channel_id=1, source_target_pairs={{8,16},{16,8},{9,17},{17,9},{10,18},{18,10},{11,19},{19,11},{12,20... | collective-permute-start | bytes 1572872 | tf_op jit(solution)/shard_map/ppermute | solution.py:31
  60.9 10.8 %collective-permute-start.6 = (f32[512,256]{1,0:T(8,128)S(1)}, f32[512,256]{1,0:T(8,128)S(1)}, u32[]{:S(2)}, u32[]{:S(2)}) collective-permute-start(f32[512,256]{1,0:T(8,128)S(1)} %get-tuple-element.51.refs_2_), channel_id=1, source_target_pairs={{0,1},{1,0},{2,3},{3,2},{4,5},{5,4},{6,7},{7,6},{8,9},{9,8},{10,11... | collective-permute-start | bytes 1572872 | tf_op jit(solution)/shard_map/ppermute | solution.py:31
  61.0 10.8 %collective-permute-start.7 = (f32[512,256]{1,0:T(8,128)S(1)}, f32[512,256]{1,0:T(8,128)S(1)}, u32[]{:S(2)}, u32[]{:S(2)}) collective-permute-start(f32[512,256]{1,0:T(8,128)S(1)} %get-tuple-element.52.refs_3_), channel_id=1, source_target_pairs={{1,2},{2,1},{3,4},{4,3},{5,6},{6,5},{9,10},{10,9},{11,12},{12,11},... | collective-permute-start | bytes 1572872 | tf_op jit(solution)/shard_map/ppermute | solution.py:31
  71.8 3.4 %copy-start.1 = (bf16[1,2048,2048]{2,1,0:T(8,128)(2,1)S(1)}, bf16[1,2048,2048]{2,1,0:T(8,128)(2,1)}, u32[]{:S(2)}) copy-start(bf16[1,2048,2048]{2,1,0:T(8,128)(2,1)} %param.10) | copy-start | bytes 25165828
  78.8 11.4 %collective-permute-start.8 = (f32[512,256]{1,0:T(8,128)S(1)}, f32[512,256]{1,0:T(8,128)S(1)}, u32[]{:S(2)}, u32[]{:S(2)}) collective-permute-start(f32[512,256]{1,0:T(8,128)S(1)} %get-tuple-element.53.refs_0_.refs_11_), channel_id=1, source_target_pairs={{0,8},{8,0},{16,24},{24,16},{1,9},{9,1},{17,25},{25,17},{2,10},{10... | collective-permute-start | bytes 1572872 | tf_op jit(solution)/shard_map/ppermute | solution.py:31
  82.5 7.8 %collective-permute-start.9 = (f32[512,256]{1,0:T(8,128)S(1)}, f32[512,256]{1,0:T(8,128)S(1)}, u32[]{:S(2)}, u32[]{:S(2)}) collective-permute-start(f32[512,256]{1,0:T(8,128)S(1)} %get-tuple-element.54.refs_1_.refs_12_), channel_id=1, source_target_pairs={{8,16},{16,8},{9,17},{17,9},{10,18},{18,10},{11,19},{19,11},{12,20... | collective-permute-start | bytes 1572872 | tf_op jit(solution)/shard_map/ppermute | solution.py:31
  83.2 7.1 %collective-permute-start.10 = (f32[512,256]{1,0:T(8,128)S(1)}, f32[512,256]{1,0:T(8,128)S(1)}, u32[]{:S(2)}, u32[]{:S(2)}) collective-permute-start(f32[512,256]{1,0:T(8,128)S(1)} %get-tuple-element.55.refs_2_.refs_13_), channel_id=1, source_target_pairs={{0,1},{1,0},{2,3},{3,2},{4,5},{5,4},{6,7},{7,6},{8,9},{9,8},{10,11... | collective-permute-start | bytes 1572872 | tf_op jit(solution)/shard_map/ppermute | solution.py:31
  88.6 1.7 collective-permute-start.11
  117.0 28.2 %slice-start = ((s8[8388608]{0:T(1024)(128)(4,1)}), s8[4194304]{0:T(1024)(128)(4,1)S(1)}, s32[]{:S(2)}) async-start(s8[8388608]{0:T(1024)(128)(4,1)} %bitcast.22), calls=%async_computation.2 | async-start | bytes 8388608
  129.4 15.8 %slice-start.1 = ((s8[8388608]{0:T(1024)(128)(4,1)}), s8[4194304]{0:T(1024)(128)(4,1)S(1)}, s32[]{:S(2)}) async-start(s8[8388608]{0:T(1024)(128)(4,1)} %bitcast.22), calls=%async_computation.3 | async-start | bytes 8388608
  132.3 12.9 %collective-permute-start.12 = (f32[512,256]{1,0:T(8,128)S(1)}, f32[512,256]{1,0:T(8,128)S(1)}, u32[]{:S(2)}, u32[]{:S(2)}) collective-permute-start(f32[512,256]{1,0:T(8,128)S(1)} %get-tuple-element.61.refs_0_), channel_id=1, source_target_pairs={{0,8},{8,0},{16,24},{24,16},{1,9},{9,1},{17,25},{25,17},{2,10},{10... | collective-permute-start | bytes 1572872 | tf_op jit(solution)/shard_map/ppermute | solution.py:31
  133.0 12.1 %collective-permute-start.13 = (f32[512,256]{1,0:T(8,128)S(1)}, f32[512,256]{1,0:T(8,128)S(1)}, u32[]{:S(2)}, u32[]{:S(2)}) collective-permute-start(f32[512,256]{1,0:T(8,128)S(1)} %get-tuple-element.62.refs_1_), channel_id=1, source_target_pairs={{8,16},{16,8},{9,17},{17,9},{10,18},{18,10},{11,19},{19,11},{12,20... | collective-permute-start | bytes 1572872 | tf_op jit(solution)/shard_map/ppermute | solution.py:31
  133.7 11.5 %collective-permute-start.14 = (f32[512,256]{1,0:T(8,128)S(1)}, f32[512,256]{1,0:T(8,128)S(1)}, u32[]{:S(2)}, u32[]{:S(2)}) collective-permute-start(f32[512,256]{1,0:T(8,128)S(1)} %get-tuple-element.63.refs_2_), channel_id=1, source_target_pairs={{0,1},{1,0},{2,3},{3,2},{4,5},{5,4},{6,7},{7,6},{8,9},{9,8},{10,11... | collective-permute-start | bytes 1572872 | tf_op jit(solution)/shard_map/ppermute | solution.py:31
  133.8 11.4 %collective-permute-start.15 = (f32[512,256]{1,0:T(8,128)S(1)}, f32[512,256]{1,0:T(8,128)S(1)}, u32[]{:S(2)}, u32[]{:S(2)}) collective-permute-start(f32[512,256]{1,0:T(8,128)S(1)} %get-tuple-element.64.refs_3_), channel_id=1, source_target_pairs={{1,2},{2,1},{3,4},{4,3},{5,6},{6,5},{9,10},{10,9},{11,12},{12,11},... | collective-permute-start | bytes 1572872 | tf_op jit(solution)/shard_map/ppermute | solution.py:31
  148.9 28.0 %collective-permute-start.16 = (f32[512,256]{1,0:T(8,128)S(1)}, f32[512,256]{1,0:T(8,128)S(1)}, u32[]{:S(2)}, u32[]{:S(2)}) collective-permute-start(f32[512,256]{1,0:T(8,128)S(1)} %get-tuple-element.66.refs_0_), channel_id=1, source_target_pairs={{0,8},{8,0},{16,24},{24,16},{1,9},{9,1},{17,25},{25,17},{2,10},{10... | collective-permute-start | bytes 1572872 | tf_op jit(solution)/shard_map/ppermute | solution.py:31
  152.6 24.3 %collective-permute-start.17 = (f32[512,256]{1,0:T(8,128)S(1)}, f32[512,256]{1,0:T(8,128)S(1)}, u32[]{:S(2)}, u32[]{:S(2)}) collective-permute-start(f32[512,256]{1,0:T(8,128)S(1)} %get-tuple-element.67.refs_1_), channel_id=1, source_target_pairs={{8,16},{16,8},{9,17},{17,9},{10,18},{18,10},{11,19},{19,11},{12,20... | collective-permute-start | bytes 1572872 | tf_op jit(solution)/shard_map/ppermute | solution.py:31
  153.3 23.6 %collective-permute-start.18 = (f32[512,256]{1,0:T(8,128)S(1)}, f32[512,256]{1,0:T(8,128)S(1)}, u32[]{:S(2)}, u32[]{:S(2)}) collective-permute-start(f32[512,256]{1,0:T(8,128)S(1)} %get-tuple-element.68.refs_2_), channel_id=1, source_target_pairs={{0,1},{1,0},{2,3},{3,2},{4,5},{5,4},{6,7},{7,6},{8,9},{9,8},{10,11... | collective-permute-start | bytes 1572872 | tf_op jit(solution)/shard_map/ppermute | solution.py:31
  156.7 20.2 %collective-permute-start.19 = (f32[512,256]{1,0:T(8,128)S(1)}, f32[512,256]{1,0:T(8,128)S(1)}, u32[]{:S(2)}, u32[]{:S(2)}) collective-permute-start(f32[512,256]{1,0:T(8,128)S(1)} %get-tuple-element.69.refs_3_), channel_id=1, source_target_pairs={{1,2},{2,1},{3,4},{4,3},{5,6},{6,5},{9,10},{10,9},{11,12},{12,11},... | collective-permute-start | bytes 1572872 | tf_op jit(solution)/shard_map/ppermute | solution.py:31

commit v2 on v1

--- a/solution.py
+++ b/solution.py
@@ -9,6 +9,7 @@
 
 HIGHEST = lax.Precision.HIGHEST
 EXTRA = 8
+FIRST = (0, 3)
 F32, BF16 = jnp.float32, jnp.bfloat16
 ANY = pl.BlockSpec(memory_space=pl.ANY)
 VMEM = pl.BlockSpec(memory_space=pltpu.VMEM)
@@ -27,10 +28,11 @@
 
 
 def exchange(parts):
-    return [
-        lax.ppermute(part, axis, pairs(lax.axis_size(axis), odd))
-        for part, (axis, odd) in zip(parts, (("grp", 0), ("grp", 1), ("cell", 0), ("cell", 1)))
-    ]
+    got = [None] * 4
+    for slot in range(4):
+        axis, odd = ("grp", "cell")[slot // 2], slot % 2
+        got[slot] = lax.ppermute(parts[slot], axis, pairs(lax.axis_size(axis), odd))
+    return got
 
 
 def slots():
@@ -77,7 +79,7 @@
     )
 
 
-def call(kernel, inputs, specs, outs, out_specs, scratch, flops):
+def call(kernel, inputs, specs, outs, out_specs, scratch, flops, limit=12 * 2**20):
     moved = sum(a.size * a.dtype.itemsize for a in inputs)
     return pl.pallas_call(
         kernel,
@@ -85,7 +87,7 @@
         in_specs=specs,
         out_specs=out_specs,
         scratch_shapes=scratch,
-        compiler_params=pltpu.CompilerParams(vmem_limit_bytes=24 * 2**20),
+        compiler_params=pltpu.CompilerParams(vmem_limit_bytes=limit),
         cost_estimate=pl.CostEstimate(flops=flops, bytes_accessed=moved // 8, transcendentals=0),
     )(*inputs)
 
@@ -120,26 +122,59 @@
     )
 
 
+def assembled_first(own, got, orders):
+    size, columns = own[0].shape
+    count = len(FIRST)
+
+    def kernel(*refs):
+        faces, _ = slots()
+        for k, s in enumerate(FIRST):
+            refs[-1][k] = refs[k][...] + exact(refs[2 * count][faces[s]], refs[count + k][...])
+
+    return call(
+        kernel,
+        [own[s] for s in FIRST] + [got[s] for s in FIRST] + [orders],
+        [VMEM] * (2 * count + 1),
+        shape(count, size, columns),
+        VMEM,
+        [],
+        2 * 2 * count * size * columns * size,
+    )
+
+
+def assembled(s, first_ref, own_refs, got_refs, order_ref, face):
+    if s in FIRST:
+        return first_ref[FIRST.index(s)]
+    return own_refs[s][...] + exact(order_ref[face], got_refs[s][...])
+
+
 def gather_primal(own, got, orders, basis, tail):
     size, columns = own[0].shape
     prim = basis.shape[0]
     whole = (4 * size, columns)
 
-    def kernel(*refs):
-        own_refs, got_refs, (order_ref, basis_ref, tail_ref) = refs[:4], refs[4:8], refs[8:11]
-        full_ref, half_ref, sent_ref = refs[11:]
+    first = assembled_first(own, got, orders)
+    last = [s for s in range(4) if s not in FIRST]
+    own, got = [own[s] for s in last], [got[s] for s in last]
+    count = len(last)
+
+    def kernel(first_ref, *refs):
+        spread = lambda part: {s: part[i] for i, s in enumerate(last)}
+        own_refs, got_refs = spread(refs[:count]), spread(refs[count : 2 * count])
+        refs = refs[2 * count :]
+        order_ref, basis_ref, tail_ref, full_ref, half_ref, sent_ref = refs
         faces, weights = slots()
         sent_ref[prim:, :] = tail_ref[...]
         for s in range(4):
-            full = own_refs[s][...] + exact(order_ref[faces[s]], got_refs[s][...])
+            full = assembled(s, first_ref, own_refs, got_refs, order_ref, faces[s])
             full_ref[s] = full
             half_ref[rows_of(faces[s], size), :] = (full * weights[s]).astype(BF16)
         sent_ref[:prim, :] = wide(basis_ref[...], half_ref[...])
 
     return call(
         kernel,
-        [*own, *got, orders, basis, tail],
-        [VMEM] * 11,
+        [first, *own, *got, orders, basis, tail],
+        [VMEM] * (4 + 2 * count),
         [
             shape(4, size, columns),
             jax.ShapeDtypeStruct(whole, BF16),
@@ -159,6 +194,7 @@
         self.at_lift = self.at_inverse + owned * self.inverse_pieces
         self.at_index = self.at_lift + owned // self.lift_pieces
         self.columns = columns
+        self.room = 10 * 2**20 + 32 * unknowns * unknowns
 
     def tail(self, inverse, lift, index):
         index = jnp.pad(index.astype(F32), ((0, 7), (0, self.columns - self.prim)))
@@ -210,6 +246,7 @@
         [VMEM] * 3,
         [],
         0,
+        level.room,
     )
 
 
@@ -242,6 +279,7 @@
         VMEM,
         [],
         0,
+        level.room,
     )
 
 
@@ -308,21 +346,29 @@
     )
 
 
-def image_of(own, got, orders, matrix, residual, past):
+def image_of(own, got, orders, matrix, residual, past, pieces):
     size, columns = own[0].shape
     n = 4 * size
     extra = len(past)
 
-    def kernel(*refs):
-        own_refs, got_refs, (order_ref, matrix_ref, residual_ref) = refs[:4], refs[4:8], refs[8:11]
-        past_refs, refs = refs[11 : 11 + extra], refs[11 + extra :]
+    first = assembled_first(own, got, orders)
+    last = [s for s in range(4) if s not in FIRST]
+    own, got = [own[s] for s in last], [got[s] for s in last]
+    count = len(last)
+
+    def kernel(first_ref, *refs):
+        spread = lambda part: {s: part[i] for i, s in enumerate(last)}
+        own_refs, got_refs = spread(refs[:count]), spread(refs[count : 2 * count])
+        refs = refs[2 * count :]
+        order_ref, matrix_ref, residual_ref = refs[:3]
+        past_refs, refs = refs[3 : 3 + extra], refs[3 + extra :]
         search_ref, outs, sums_ref, half_ref = refs[0], refs[1:5], refs[5], refs[6]
         faces, weights = slots()
         for s in range(4):
-            search = own_refs[s][...] + exact(order_ref[faces[s]], got_refs[s][...])
+            search = assembled(s, first_ref, own_refs, got_refs, order_ref, faces[s])
             search_ref[s] = search
             half_ref[rows_of(faces[s], size), :] = search.astype(BF16)
-        sums = [jnp.zeros((1, columns), F32) for _ in range(3)]
+        sums = [jnp.zeros((1, columns), F32) for _ in range(4)]
         for s in range(4):
             image = wide(matrix_ref[rows_of(faces[s], size), :], half_ref[...])
             outs[s][...] = image
@@ -331,13 +377,19 @@
             sums[1] += column_sums(search * image)
             if extra:
                 sums[2] += column_sums(search * past_refs[s][...])
-        sums_ref[...] = jnp.concatenate(sums + [jnp.zeros((EXTRA - 3, columns), F32)], axis=0)
-
-    return call(
-        kernel,
-        [*own, *got, orders, matrix, residual, *past],
-        [VMEM] * (11 + extra),
-        [shape(4, size, columns)] + [shape(size, columns)] * 4 + [shape(EXTRA, columns)],
+        sums = stacked(jnp.concatenate(sums, axis=0), pieces)
+        rows = sums.shape[0]
+        sums_ref[:rows, :] = sums
+        if rows < EXTRA:
+            sums_ref[rows:, :] = jnp.zeros((EXTRA - rows, columns // pieces), F32)
+
+    return call(
+        kernel,
+        [first, *own, *got, orders, matrix, residual, *past],
+        [VMEM] * (4 + 2 * count + extra),
+        [shape(4, size, columns)]
+        + [shape(size, columns)] * 4
+        + [shape(EXTRA, columns // pieces)],
         [VMEM] * 6,
         [pltpu.VMEM((n, columns), BF16)],
         2 * n * columns * (n + 2 * size),
@@ -347,6 +399,7 @@
 def finish(own, got, orders, search, second, residual, image, total, sums):
     size, columns = own[0].shape
     n = 4 * size
+    pieces = columns // sums.shape[2]
 
     def kernel(*refs):
         own_refs, got_refs, order_ref = refs[:4], refs[4:8], refs[8]
@@ -354,7 +407,7 @@
         out_refs, (solution_buf, residual_buf, sems) = refs[15:17], refs[17:]
         faces, _ = slots()
         product, curvature = total_ref[0:1, :], total_ref[1:2, :]
-        sums = jnp.sum(sums_ref[...], axis=0)
+        sums = beside(jnp.sum(sums_ref[...], axis=0)[: 4 * pieces], pieces)
         alpha = product / curvature
         beta = sums[0:1] / product
         alpha_next = sums[0:1] / (sums[1:2] + beta * (2.0 * sums[2:3] + beta * curvature))
@@ -420,15 +473,17 @@
     sent, picked, up = lower_first(level, gathered, index, coarsest_inverse)
     ups = lax.all_gather(sent, "grp", axis=0, tiled=False)
     *own, picked = solve_first(half, local_inverse, lift, picked, up, ups)
-    search, *own, sums = image_of(own, exchange(own), orders, schur, residual, ())
+    search, *own, sums = image_of(own, exchange(own), orders, schur, residual, (), 1)
     image, _, sent = gather_primal(own, exchange(own), orders, basis, sums)
     again = lax.all_gather(sent, "cell", axis=0, tiled=False)
     sent = lower_second(level, gathered, index, ups, again)
     sent = lax.all_to_all(sent, "grp", 0, 0, tiled=True)
     *shared, residual, total = solve_second(residual, image, local_inverse, lift, picked, sent)
-    second, *own, sums = image_of(shared, exchange(shared), orders, schur, residual, own)
-    sums = jnp.broadcast_to(sums[None], (groups * cells, EXTRA, columns))
+    second, *own, sums = image_of(
+        shared, exchange(shared), orders, schur, residual, own, max(columns // 128, 1)
+    )
     got = exchange(own)
+    sums = jnp.broadcast_to(sums[None], (groups * cells,) + sums.shape)
     sums = lax.all_to_all(sums, ("grp", "cell"), 0, 0, tiled=True)
     result, residual = finish(own, got, orders, search, second, residual, image, total, sums)
     return result[None], residual[None]

time: 181 us -> 171 us (0.945)
  blocking collectives: 88.8 us -> 74.7 us
  local copies, waits for them, and re-layouts: 5.39 us -> 2.01 us
  starting transfers between devices: 29.6 us -> 32.6 us
  waiting for transfers between devices: 29.8 us -> 31.9 us
  Pallas kernels: 25.3 us -> 27.2 us
    all_gather x1, blocking collectives: 24.3 us -> 13.5 us  [body(): again = lax.all_gather(sent, 'cell', axis=0, tiled=False)]
    unnamed x23, local copies, waits for them, and re-layouts: 5.28 us -> 1.91 us
    ppermute x20, starting transfers between devices: 29.6 us -> 32.6 us  [exchange(): got[slot] = lax.ppermute(parts[slot], axis, pairs(lax.axis_size(axis), odd))]
    all_to_all x1, blocking collectives: 19.5 us -> 17.2 us  [body(): sums = lax.all_to_all(sums, ('grp', 'cell'), 0, 0, tiled=True)]
    all_gather x1, blocking collectives: 16.6 us -> 14.5 us  [body(): gathered = lax.all_gather(sent, 'cell', axis=0, tiled=False)]
    ppermute x20, waiting for transfers between devices: 29.8 us -> 31.9 us  [exchange(): got[slot] = lax.ppermute(parts[slot], axis, pairs(lax.axis_size(axis), odd))]
    pallas_call x10 -> x14, Pallas kernels: 25.3 us -> 27.2 us  [call(): pl.pallas_call(kernel, out_shape=outs, in_specs=specs, out_specs=out_spec...]
    all_gather x1, blocking collectives: 17.4 us -> 19.2 us  [body(): ups = lax.all_gather(sent, 'grp', axis=0, tiled=False)]
  transfers between devices with their start and end apart: 20 -> 20, of which waited for: 4 -> 4; matrix products, arithmetic and copies ran while one was open for 1% -> 1% of each run, Pallas kernels for 0% -> 2%
where the time goes in v2:
time: 171 us; the launch traced here: 170 us
  blocking collectives  74.7 us (44%)
  starting transfers between devices  32.6 us (19%)
  waiting for transfers between devices  31.9 us (19%)
  Pallas kernels  27.2 us (16%)
  local copies, waits for them, and re-layouts  2.01 us (1%)
    ppermute x20, starting transfers between devices, exchange(): got[slot] = lax.ppermute(parts[slot], axis, pairs(lax.axis_size(axis), odd))  32.6 us
    ppermute x20, waiting for transfers between devices, exchange(): got[slot] = lax.ppermute(parts[slot], axis, pairs(lax.axis_size(axis), odd))  31.9 us
    pallas_call x14, Pallas kernels, call(): pl.pallas_call(kernel, out_shape=outs, in_specs=specs, out_specs=out_spec...  27.2 us
    all_gather x1, blocking collectives, body(): ups = lax.all_gather(sent, 'grp', axis=0, tiled=False)  19.2 us
    all_to_all x1, blocking collectives, body(): sums = lax.all_to_all(sums, ('grp', 'cell'), 0, 0, tiled=True)  17.2 us
    all_gather x1, blocking collectives, body(): gathered = lax.all_gather(sent, 'cell', axis=0, tiled=False)  14.5 us
    all_gather x1, blocking collectives, body(): again = lax.all_gather(sent, 'cell', axis=0, tiled=False)  13.5 us
    all_to_all x1, blocking collectives, body(): sent = lax.all_to_all(sent, 'grp', 0, 0, tiled=True)  10.3 us
  transfers between devices with their start and end apart: 20, of which 4 were waited for; matrix products, arithmetic and copies ran while one was open for 1% of the time, Pallas kernels for 2%

profile of v2, /device:TPU:0, one launch (start us, length us, event | category | flops | bytes accessed | tf_op | source)
XLA Modules:
  0.0 170.1 jit_solution(11237939230688352126)
XLA Ops:
  0.7 1.6 copy-done
  2.3 1.0 shard_map.104
  3.3 3.1 %collective-permute-start = (f32[512,256]{1,0:T(8,128)S(1)}, f32[512,256]{1,0:T(8,128)S(1)}, u32[]{:S(2)}, u32[]{:S(2)}) collective-permute-start(f32[512,256]{1,0:T(8,128)S(1)} %get-tuple-element.39.refs_0_), channel_id=1, source_target_pairs={{0,8},{8,0},{16,24},{24,16},{1,9},{9,1},{17,25},{25,17},{2,10},{10... | collective-permute-start | bytes 1572872 | tf_op jit(solution)/shard_map/ppermute | solution.py:34
  6.3 0.7 collective-permute-start.1
  7.0 1.5 collective-permute-start.2
  8.5 2.8 %collective-permute-start.3 = (f32[512,256]{1,0:T(8,128)}, f32[512,256]{1,0:T(8,128)}, u32[]{:S(2)}, u32[]{:S(2)}) collective-permute-start(f32[512,256]{1,0:T(8,128)} %get-tuple-element.42.refs_1_), channel_id=1, source_target_pairs={{0,1},{1,0},{2,3},{3,2},{4,5},{5,4},{6,7},{7,6},{8,9},{9,8},{10,11... | collective-permute-start | bytes 1572872 | tf_op jit(solution)/shard_map/ppermute | solution.py:34
  11.3 0.1 copy.13.index_ref
  11.4 0.3 copy.11
  11.8 0.5 fusion.refs_4_.refs_8_
  12.3 6.0 %collective-permute-done.refs_2_ = f32[512,256]{1,0:T(8,128)S(1)} collective-permute-done((f32[512,256]{1,0:T(8,128)S(1)}, f32[512,256]{1,0:T(8,128)S(1)}, u32[]{:S(2)}, u32[]{:S(2)}) %collective-permute-start) | collective-permute-done | bytes 524320 | tf_op jit(solution)/shard_map/ppermute | solution.py:34
  18.3 0.7 shard_map.105.first_ref
  19.1 0.0 slice-start.1
  19.1 2.8 %shard_map.106 = (f32[4,512,256]{2,1,0:T(8,128)S(1)}, bf16[2048,256]{1,0:T(8,128)(2,1)S(1)}, f32[88,256]{1,0:T(8,128)S(1)}) custom-call(f32[2,512,256]{2,1,0:T(8,128)S(1)} %shard_map.105.first_ref, f32[512,256]{1,0:T(8,128)S(1)} %get-tuple-element.41.refs_0_, f32[512,256]{1,0:T(8,128)} %get-tuple-element.42.refs_1_, ...), custom_call_target="tpu_custom_call" | custom-call | flops 1107296256 | bytes 678912 | tf_op jit(solution)/shard_map/pallas_call | solution.py:84
  21.8 14.5 %all-gather = f32[704,256]{1,0:T(8,128)S(1)} all-gather(f32[88,256]{1,0:T(8,128)S(1)} %get-tuple-element.45), channel_id=2, replica_groups=mesh['grp'=4,'cell'=8] {'cell'}, dimensions={0}, use_global_device_ids=true | all-gather | bytes 811008 | tf_op jit(solution)/shard_map/all_gather | solution.py:472
  36.3 1.1 shard_map.107
  37.4 19.2 %all-gather.1 = f32[576,256]{1,0:T(8,128)S(1)} all-gather(f32[144,256]{1,0:T(8,128)S(1)} %get-tuple-element.48), channel_id=3, replica_groups=mesh['grp'=4,'cell'=8] {'grp'}, dimensions={0}, use_global_device_ids=true | all-gather | bytes 737280 | tf_op jit(solution)/shard_map/all_gather | solution.py:474
  56.7 3.1 %shard_map.108 = (f32[512,256]{1,0:T(8,128)S(1)}, f32[512,256]{1,0:T(8,128)S(1)}, f32[512,256]{1,0:T(8,128)S(1)}, f32[512,256]{1,0:T(8,128)S(1)}, f32[32,256]{1,0:T(8,128)S(1)}) custom-call(bf16[2048,256]{1,0:T(8,128)(2,1)S(1)} %get-tuple-element.44.half_ref, bf16[2048,2048]{1,0:T(8,128)(2,1)S(1)} %bitcast.21, bf16[2048,32]{1,0:T(8,128)(2,1)S(1)} %bitcast.31, ...), custom_call_target="tpu_custom_call" | custom-call | flops 2147483648 | bytes 1275904 | tf_op jit(solution)/shard_map/pallas_call | solution.py:84
  59.8 0.1 collective-permute-start.4
  59.9 0.7 collective-permute-start.5
  60.6 0.7 collective-permute-start.6
  61.3 1.8 %collective-permute-start.7 = (f32[512,256]{1,0:T(8,128)S(1)}, f32[512,256]{1,0:T(8,128)S(1)}, u32[]{:S(2)}, u32[]{:S(2)}) collective-permute-start(f32[512,256]{1,0:T(8,128)S(1)} %get-tuple-element.52.refs_1_), channel_id=1, source_target_pairs={{0,1},{1,0},{2,3},{3,2},{4,5},{5,4},{6,7},{7,6},{8,9},{9,8},{10,11... | collective-permute-start | bytes 1572872 | tf_op jit(solution)/shard_map/ppermute | solution.py:34
  63.1 8.6 %collective-permute-done.4.refs_2_ = f32[512,256]{1,0:T(8,128)S(1)} collective-permute-done((f32[512,256]{1,0:T(8,128)S(1)}, f32[512,256]{1,0:T(8,128)S(1)}, u32[]{:S(2)}, u32[]{:S(2)}) %collective-permute-start.4) | collective-permute-done | bytes 524320 | tf_op jit(solution)/shard_map/ppermute | solution.py:34
  71.7 0.7 shard_map.109.first_ref
  72.5 3.1 %shard_map.110 = (f32[4,512,256]{2,1,0:T(8,128)S(1)}, f32[512,256]{1,0:T(8,128)S(1)}, f32[512,256]{1,0:T(8,128)S(1)}, f32[512,256]{1,0:T(8,128)S(1)}, f32[512,256]{1,0:T(8,128)S(1)}, /*index=5*/f32[8,256]{1,0:T(8,128)S(1)}) custom-call(f32[2,512,256]{2,1,0:T(8,128)S(1)} %shard_map.109.first_ref, f32[512,256]{1,0:T(8,128)S(1)} %get-tuple-element.51.refs_0_, ...), custom_call_target="tpu_custom_call" | custom-call | flops 3221225472 | bytes 1966080 | tf_op jit(solution)/shard_map/pallas_call | solution.py:84
  75.6 6.2 %collective-permute-start.8 = (f32[512,256]{1,0:T(8,128)S(1)}, f32[512,256]{1,0:T(8,128)S(1)}, u32[]{:S(2)}, u32[]{:S(2)}) collective-permute-start(f32[512,256]{1,0:T(8,128)S(1)} %get-tuple-element.53.refs_0_.refs_7_), channel_id=1, source_target_pairs={{0,8},{8,0},{16,24},{24,16},{1,9},{9,1},{17,25},{25,17},{2,10},{10... | collective-permute-start | bytes 1572872 | tf_op jit(solution)/shard_map/ppermute | solution.py:34
  81.8 0.7 collective-permute-start.9
  82.5 0.7 collective-permute-start.10
  83.2 3.2 %collective-permute-start.11 = (f32[512,256]{1,0:T(8,128)S(1)}, f32[512,256]{1,0:T(8,128)S(1)}, u32[]{:S(2)}, u32[]{:S(2)}) collective-permute-start(f32[512,256]{1,0:T(8,128)S(1)} %get-tuple-element.56.refs_1_.refs_9_), channel_id=1, source_target_pairs={{0,1},{1,0},{2,3},{3,2},{4,5},{5,4},{6,7},{7,6},{8,9},{9,8},{10,11... | collective-permute-start | bytes 1572872 | tf_op jit(solution)/shard_map/ppermute | solution.py:34
  86.4 8.0 %collective-permute-done.8.refs_2_ = f32[512,256]{1,0:T(8,128)S(1)} collective-permute-done((f32[512,256]{1,0:T(8,128)S(1)}, f32[512,256]{1,0:T(8,128)S(1)}, u32[]{:S(2)}, u32[]{:S(2)}) %collective-permute-start.8) | collective-permute-done | bytes 524320 | tf_op jit(solution)/shard_map/ppermute | solution.py:34
  94.4 0.7 shard_map.111.first_ref
  95.2 2.0 %shard_map.112 = (f32[4,512,256]{2,1,0:T(8,128)S(1)}, bf16[2048,256]{1,0:T(8,128)(2,1)}, f32[40,256]{1,0:T(8,128)S(1)}) custom-call(f32[2,512,256]{2,1,0:T(8,128)S(1)} %shard_map.111.first_ref, f32[512,256]{1,0:T(8,128)S(1)} %get-tuple-element.55.refs_0_.refs_8_, f32[512,256]{1,0:T(8,128)S(1)} %get-tuple-element.56.refs_1_.refs_9_, ...), custom_call_target="tpu_custom_call" | custom-call | flops 1107296256 | bytes 672768 | tf_op jit(solution)/shard_map/pallas_call | solution.py:84
  97.1 13.5 %all-gather.2 = f32[320,256]{1,0:T(8,128)S(1)} all-gather(f32[40,256]{1,0:T(8,128)S(1)} %get-tuple-element.60), channel_id=4, replica_groups=mesh['grp'=4,'cell'=8] {'cell'}, dimensions={0}, use_global_device_ids=true | all-gather | bytes 368640 | tf_op jit(solution)/shard_map/all_gather | solution.py:478
  110.6 1.4 shard_map.113
  112.0 10.3 %all_to_all.10.sent_ref = f32[4,40,256]{2,1,0:T(8,128)S(1)} all-to-all(f32[4,40,256]{2,1,0:T(8,128)S(1)} %shard_map.113), channel_id=1, replica_groups=mesh['grp'=4,'cell'=8] {'grp'}, dimensions={0} | all-to-all | bytes 327680 | tf_op jit(solution)/shard_map/all_to_all | solution.py:480
  122.3 2.9 %shard_map.114 = (f32[512,256]{1,0:T(8,128)S(1)}, f32[512,256]{1,0:T(8,128)S(1)}, f32[512,256]{1,0:T(8,128)S(1)}, f32[512,256]{1,0:T(8,128)S(1)}, f32[4,512,256]{2,1,0:T(8,128)S(1)}, /*index=5*/f32[8,256]{1,0:T(8,128)S(1)}) custom-call(f32[4,512,256]{2,1,0:T(8,128)S(1)} %get-tuple-element.43.refs_6_.residual_ref, ...), custom_call_target="tpu_custom_call" | custom-call | flops 2147483648 | bytes 1613824 | tf_op jit(solution)/shard_map/pallas_call | solution.py:84
  125.2 0.7 collective-permute-start.12
  125.9 0.7 collective-permute-start.13
  126.6 0.7 collective-permute-start.14
  127.3 1.5 collective-permute-start.15
  128.8 9.3 %collective-permute-done.12.refs_2_ = f32[512,256]{1,0:T(8,128)S(1)} collective-permute-done((f32[512,256]{1,0:T(8,128)S(1)}, f32[512,256]{1,0:T(8,128)S(1)}, u32[]{:S(2)}, u32[]{:S(2)}) %collective-permute-start.12) | collective-permute-done | bytes 524320 | tf_op jit(solution)/shard_map/ppermute | solution.py:34
  138.0 0.8 shard_map.115.first_ref
  138.8 3.2 %shard_map.116 = (f32[4,512,256]{2,1,0:T(8,128)S(1)}, f32[512,256]{1,0:T(8,128)S(1)}, f32[512,256]{1,0:T(8,128)S(1)}, f32[512,256]{1,0:T(8,128)S(1)}, f32[512,256]{1,0:T(8,128)S(1)}, /*index=5*/f32[8,128]{1,0:T(8,128)S(1)}) custom-call(f32[2,512,256]{2,1,0:T(8,128)S(1)} %shard_map.115.first_ref, f32[512,256]{1,0:T(8,128)S(1)} %get-tuple-element.63.refs_0_, ...), custom_call_target="tpu_custom_call" | custom-call | flops 3221225472 | bytes 2228224 | tf_op jit(solution)/shard_map/pallas_call | solution.py:84
  142.1 5.5 %collective-permute-start.16 = (f32[512,256]{1,0:T(8,128)S(1)}, f32[512,256]{1,0:T(8,128)S(1)}, u32[]{:S(2)}, u32[]{:S(2)}) collective-permute-start(f32[512,256]{1,0:T(8,128)S(1)} %get-tuple-element.66.refs_0_), channel_id=1, source_target_pairs={{0,8},{8,0},{16,24},{24,16},{1,9},{9,1},{17,25},{25,17},{2,10},{10... | collective-permute-start | bytes 1572872 | tf_op jit(solution)/shard_map/ppermute | solution.py:34
  147.6 0.7 collective-permute-start.17
  148.3 0.1 collective-permute-start.18
  148.4 0.7 collective-permute-start.19
  149.1 17.2 %all_to_all.11.refs_14_ = f32[32,8,128]{2,1,0:T(8,128)S(1)} all-to-all(f32[32,8,128]{2,1,0:T(8,128)S(1)} %broadcast_in_dim.6), channel_id=1, replica_groups=mesh['grp'=4,'cell'=8] {'grp','cell'}, dimensions={0} | all-to-all | bytes 262144 | tf_op jit(solution)/shard_map/all_to_all | solution.py:487
  166.4 3.5 %shard_map.117 = (f32[2048,256]{1,0:T(8,128)}, f32[2048,256]{1,0:T(8,128)}) custom-call(f32[512,256]{1,0:T(8,128)S(1)} %get-tuple-element.66.refs_0_, f32[512,256]{1,0:T(8,128)S(1)} %get-tuple-element.67.refs_1_, f32[512,256]{1,0:T(8,128)S(1)} %get-tuple-element.68.refs_2_, f32[512,256]{1,0:T(8,128)S(1)} %get-tuple-element.69.refs_3_, ...), custom_call_target="tpu_custom_call" | custom-call | flops 1073741824 | bytes 1852416 | tf_op jit(solution)/shard_map/pallas_call | solution.py:84
  (42 shorter events, 0.1 us)
Async XLA Ops:
  0.6 10.7 %copy-start.6 = (s32[1,32]{1,0:T(1,128)S(1)}, s32[1,32]{1,0:T(1,128)}, u32[]{:S(2)}) copy-start(s32[1,32]{1,0:T(1,128)} %param.14) | copy-start | bytes 388
  0.6 1.6 copy-start
  2.2 9.1 %copy-start.4 = (f32[1,32,128]{2,1,0:T(8,128)S(1)}, f32[1,32,128]{2,1,0:T(8,128)}, u32[]{:S(2)}) copy-start(f32[1,32,128]{2,1,0:T(8,128)} %param.16) | copy-start | bytes 49156
  2.2 9.2 %copy-start.1 = (bf16[1,32,2048]{2,1,0:T(8,128)(2,1)S(1)}, bf16[1,32,2048]{2,1,0:T(8,128)(2,1)}, u32[]{:S(2)}) copy-start(bf16[1,32,2048]{2,1,0:T(8,128)(2,1)} %param.13) | copy-start | bytes 393220
  2.2 9.5 %copy-start.3 = (f32[1,32,256]{2,1,0:T(8,128)S(1)}, f32[1,32,256]{2,1,0:T(8,128)}, u32[]{:S(2)}) copy-start(f32[1,32,256]{2,1,0:T(8,128)} %param.15) | copy-start | bytes 98308
  2.2 9.5 %copy-start.5 = (s32[1,4,512]{2,1,0:T(4,128)S(1)}, s32[1,4,512]{2,1,0:T(4,128)}, u32[]{:S(2)}) copy-start(s32[1,4,512]{2,1,0:T(4,128)} %param.12) | copy-start | bytes 24580
  3.3 15.0 %collective-permute-start = (f32[512,256]{1,0:T(8,128)S(1)}, f32[512,256]{1,0:T(8,128)S(1)}, u32[]{:S(2)}, u32[]{:S(2)}) collective-permute-start(f32[512,256]{1,0:T(8,128)S(1)} %get-tuple-element.39.refs_0_), channel_id=1, source_target_pairs={{0,8},{8,0},{16,24},{24,16},{1,9},{9,1},{17,25},{25,17},{2,10},{10... | collective-permute-start | bytes 1572872 | tf_op jit(solution)/shard_map/ppermute | solution.py:34
  6.3 11.9 %collective-permute-start.1 = (f32[512,256]{1,0:T(8,128)S(1)}, f32[512,256]{1,0:T(8,128)S(1)}, u32[]{:S(2)}, u32[]{:S(2)}) collective-permute-start(f32[512,256]{1,0:T(8,128)S(1)} %get-tuple-element.40.refs_1_), channel_id=1, source_target_pairs={{1,2},{2,1},{3,4},{4,3},{5,6},{6,5},{9,10},{10,9},{11,12},{12,11},... | collective-permute-start | bytes 1572872 | tf_op jit(solution)/shard_map/ppermute | solution.py:34
  7.0 12.0 %collective-permute-start.2 = (f32[512,256]{1,0:T(8,128)S(1)}, f32[512,256]{1,0:T(8,128)}, u32[]{:S(2)}, u32[]{:S(2)}) collective-permute-start(f32[512,256]{1,0:T(8,128)S(1)} %get-tuple-element.41.refs_0_), channel_id=1, source_target_pairs={{8,16},{16,8},{9,17},{17,9},{10,18},{18,10},{11,19},{19,11},{12,20... | collective-permute-start | bytes 1572872 | tf_op jit(solution)/shard_map/ppermute | solution.py:34
  8.5 10.5 %collective-permute-start.3 = (f32[512,256]{1,0:T(8,128)}, f32[512,256]{1,0:T(8,128)}, u32[]{:S(2)}, u32[]{:S(2)}) collective-permute-start(f32[512,256]{1,0:T(8,128)} %get-tuple-element.42.refs_1_), channel_id=1, source_target_pairs={{0,1},{1,0},{2,3},{3,2},{4,5},{5,4},{6,7},{7,6},{8,9},{9,8},{10,11... | collective-permute-start | bytes 1572872 | tf_op jit(solution)/shard_map/ppermute | solution.py:34
  11.7 44.9 %slice-start = ((s8[8388608]{0:T(1024)(128)(4,1)}), s8[4194304]{0:T(1024)(128)(4,1)S(1)}, s32[]{:S(2)}) async-start(s8[8388608]{0:T(1024)(128)(4,1)} %bitcast.19), calls=%async_computation.2 | async-start | bytes 8388608
  19.0 17.3 %copy-start.2 = (f32[128,128]{1,0:T(8,128)S(1)}, f32[128,128]{1,0:T(8,128)}, u32[]{:S(2)}) copy-start(f32[128,128]{1,0:T(8,128)} %coarsest_ref.1) | copy-start | bytes 196612
  19.1 37.6 %slice-start.1 = ((s8[8388608]{0:T(1024)(128)(4,1)}), s8[4194304]{0:T(1024)(128)(4,1)S(1)}, s32[]{:S(2)}) async-start(s8[8388608]{0:T(1024)(128)(4,1)} %bitcast.19), calls=%async_computation.3 | async-start | bytes 8388608
  37.4 35.0 %slice-start.2 = ((s8[8388608]{0:T(1024)(128)(4,1)}), s8[4194304]{0:T(1024)(128)(4,1)S(1)}, s32[]{:S(2)}) async-start(s8[8388608]{0:T(1024)(128)(4,1)} %bitcast.23), calls=%async_computation.4 | async-start | bytes 8388608
  56.7 15.8 %slice-start.3 = ((s8[8388608]{0:T(1024)(128)(4,1)}), s8[4194304]{0:T(1024)(128)(4,1)S(1)}, s32[]{:S(2)}) async-start(s8[8388608]{0:T(1024)(128)(4,1)} %bitcast.23), calls=%async_computation.5 | async-start | bytes 8388608
  59.8 11.8 %collective-permute-start.4 = (f32[512,256]{1,0:T(8,128)S(1)}, f32[512,256]{1,0:T(8,128)S(1)}, u32[]{:S(2)}, u32[]{:S(2)}) collective-permute-start(f32[512,256]{1,0:T(8,128)S(1)} %get-tuple-element.49.refs_0_), channel_id=1, source_target_pairs={{0,8},{8,0},{16,24},{24,16},{1,9},{9,1},{17,25},{25,17},{2,10},{10... | collective-permute-start | bytes 1572872 | tf_op jit(solution)/shard_map/ppermute | solution.py:34
  59.9 11.8 %collective-permute-start.5 = (f32[512,256]{1,0:T(8,128)S(1)}, f32[512,256]{1,0:T(8,128)S(1)}, u32[]{:S(2)}, u32[]{:S(2)}) collective-permute-start(f32[512,256]{1,0:T(8,128)S(1)} %get-tuple-element.50.refs_1_), channel_id=1, source_target_pairs={{1,2},{2,1},{3,4},{4,3},{5,6},{6,5},{9,10},{10,9},{11,12},{12,11},... | collective-permute-start | bytes 1572872 | tf_op jit(solution)/shard_map/ppermute | solution.py:34
  60.6 11.8 %collective-permute-start.6 = (f32[512,256]{1,0:T(8,128)S(1)}, f32[512,256]{1,0:T(8,128)S(1)}, u32[]{:S(2)}, u32[]{:S(2)}) collective-permute-start(f32[512,256]{1,0:T(8,128)S(1)} %get-tuple-element.51.refs_0_), channel_id=1, source_target_pairs={{8,16},{16,8},{9,17},{17,9},{10,18},{18,10},{11,19},{19,11},{12,20... | collective-permute-start | bytes 1572872 | tf_op jit(solution)/shard_map/ppermute | solution.py:34
  61.3 11.1 %collective-permute-start.7 = (f32[512,256]{1,0:T(8,128)S(1)}, f32[512,256]{1,0:T(8,128)S(1)}, u32[]{:S(2)}, u32[]{:S(2)}) collective-permute-start(f32[512,256]{1,0:T(8,128)S(1)} %get-tuple-element.52.refs_1_), channel_id=1, source_target_pairs={{0,1},{1,0},{2,3},{3,2},{4,5},{5,4},{6,7},{7,6},{8,9},{9,8},{10,11... | collective-permute-start | bytes 1572872 | tf_op jit(solution)/shard_map/ppermute | solution.py:34
  75.6 18.8 %collective-permute-start.8 = (f32[512,256]{1,0:T(8,128)S(1)}, f32[512,256]{1,0:T(8,128)S(1)}, u32[]{:S(2)}, u32[]{:S(2)}) collective-permute-start(f32[512,256]{1,0:T(8,128)S(1)} %get-tuple-element.53.refs_0_.refs_7_), channel_id=1, source_target_pairs={{0,8},{8,0},{16,24},{24,16},{1,9},{9,1},{17,25},{25,17},{2,10},{10... | collective-permute-start | bytes 1572872 | tf_op jit(solution)/shard_map/ppermute | solution.py:34
  81.8 12.6 %collective-permute-start.9 = (f32[512,256]{1,0:T(8,128)S(1)}, f32[512,256]{1,0:T(8,128)S(1)}, u32[]{:S(2)}, u32[]{:S(2)}) collective-permute-start(f32[512,256]{1,0:T(8,128)S(1)} %get-tuple-element.54.refs_1_.refs_10_), channel_id=1, source_target_pairs={{1,2},{2,1},{3,4},{4,3},{5,6},{6,5},{9,10},{10,9},{11,12},{12,11},... | collective-permute-start | bytes 1572872 | tf_op jit(solution)/shard_map/ppermute | solution.py:34
  82.5 12.7 %collective-permute-start.10 = (f32[512,256]{1,0:T(8,128)S(1)}, f32[512,256]{1,0:T(8,128)S(1)}, u32[]{:S(2)}, u32[]{:S(2)}) collective-permute-start(f32[512,256]{1,0:T(8,128)S(1)} %get-tuple-element.55.refs_0_.refs_8_), channel_id=1, source_target_pairs={{8,16},{16,8},{9,17},{17,9},{10,18},{18,10},{11,19},{19,11},{12,20... | collective-permute-start | bytes 1572872 | tf_op jit(solution)/shard_map/ppermute | solution.py:34
  83.2 12.0 %collective-permute-start.11 = (f32[512,256]{1,0:T(8,128)S(1)}, f32[512,256]{1,0:T(8,128)S(1)}, u32[]{:S(2)}, u32[]{:S(2)}) collective-permute-start(f32[512,256]{1,0:T(8,128)S(1)} %get-tuple-element.56.refs_1_.refs_9_), channel_id=1, source_target_pairs={{0,1},{1,0},{2,3},{3,2},{4,5},{5,4},{6,7},{7,6},{8,9},{9,8},{10,11... | collective-permute-start | bytes 1572872 | tf_op jit(solution)/shard_map/ppermute | solution.py:34
  125.2 12.8 %collective-permute-start.12 = (f32[512,256]{1,0:T(8,128)S(1)}, f32[512,256]{1,0:T(8,128)S(1)}, u32[]{:S(2)}, u32[]{:S(2)}) collective-permute-start(f32[512,256]{1,0:T(8,128)S(1)} %get-tuple-element.61.refs_0_), channel_id=1, source_target_pairs={{0,8},{8,0},{16,24},{24,16},{1,9},{9,1},{17,25},{25,17},{2,10},{10... | collective-permute-start | bytes 1572872 | tf_op jit(solution)/shard_map/ppermute | solution.py:34
  125.9 12.1 %collective-permute-start.13 = (f32[512,256]{1,0:T(8,128)S(1)}, f32[512,256]{1,0:T(8,128)S(1)}, u32[]{:S(2)}, u32[]{:S(2)}) collective-permute-start(f32[512,256]{1,0:T(8,128)S(1)} %get-tuple-element.62.refs_1_), channel_id=1, source_target_pairs={{1,2},{2,1},{3,4},{4,3},{5,6},{6,5},{9,10},{10,9},{11,12},{12,11},... | collective-permute-start | bytes 1572872 | tf_op jit(solution)/shard_map/ppermute | solution.py:34
  126.6 12.2 %collective-permute-start.14 = (f32[512,256]{1,0:T(8,128)S(1)}, f32[512,256]{1,0:T(8,128)S(1)}, u32[]{:S(2)}, u32[]{:S(2)}) collective-permute-start(f32[512,256]{1,0:T(8,128)S(1)} %get-tuple-element.63.refs_0_), channel_id=1, source_target_pairs={{8,16},{16,8},{9,17},{17,9},{10,18},{18,10},{11,19},{19,11},{12,20... | collective-permute-start | bytes 1572872 | tf_op jit(solution)/shard_map/ppermute | solution.py:34
  127.3 11.5 %collective-permute-start.15 = (f32[512,256]{1,0:T(8,128)S(1)}, f32[512,256]{1,0:T(8,128)S(1)}, u32[]{:S(2)}, u32[]{:S(2)}) collective-permute-start(f32[512,256]{1,0:T(8,128)S(1)} %get-tuple-element.64.refs_1_), channel_id=1, source_target_pairs={{0,1},{1,0},{2,3},{3,2},{4,5},{5,4},{6,7},{7,6},{8,9},{9,8},{10,11... | collective-permute-start | bytes 1572872 | tf_op jit(solution)/shard_map/ppermute | solution.py:34
  142.1 24.3 %collective-permute-start.16 = (f32[512,256]{1,0:T(8,128)S(1)}, f32[512,256]{1,0:T(8,128)S(1)}, u32[]{:S(2)}, u32[]{:S(2)}) collective-permute-start(f32[512,256]{1,0:T(8,128)S(1)} %get-tuple-element.66.refs_0_), channel_id=1, source_target_pairs={{0,8},{8,0},{16,24},{24,16},{1,9},{9,1},{17,25},{25,17},{2,10},{10... | collective-permute-start | bytes 1572872 | tf_op jit(solution)/shard_map/ppermute | solution.py:34
  147.6 18.7 %collective-permute-start.17 = (f32[512,256]{1,0:T(8,128)S(1)}, f32[512,256]{1,0:T(8,128)S(1)}, u32[]{:S(2)}, u32[]{:S(2)}) collective-permute-start(f32[512,256]{1,0:T(8,128)S(1)} %get-tuple-element.67.refs_1_), channel_id=1, source_target_pairs={{8,16},{16,8},{9,17},{17,9},{10,18},{18,10},{11,19},{19,11},{12,20... | collective-permute-start | bytes 1572872 | tf_op jit(solution)/shard_map/ppermute | solution.py:34
  148.3 18.0 %collective-permute-start.18 = (f32[512,256]{1,0:T(8,128)S(1)}, f32[512,256]{1,0:T(8,128)S(1)}, u32[]{:S(2)}, u32[]{:S(2)}) collective-permute-start(f32[512,256]{1,0:T(8,128)S(1)} %get-tuple-element.68.refs_2_), channel_id=1, source_target_pairs={{0,1},{1,0},{2,3},{3,2},{4,5},{5,4},{6,7},{7,6},{8,9},{9,8},{10,11... | collective-permute-start | bytes 1572872 | tf_op jit(solution)/shard_map/ppermute | solution.py:34
  148.4 18.0 %collective-permute-start.19 = (f32[512,256]{1,0:T(8,128)S(1)}, f32[512,256]{1,0:T(8,128)S(1)}, u32[]{:S(2)}, u32[]{:S(2)}) collective-permute-start(f32[512,256]{1,0:T(8,128)S(1)} %get-tuple-element.69.refs_3_), channel_id=1, source_target_pairs={{1,2},{2,1},{3,4},{4,3},{5,6},{6,5},{9,10},{10,9},{11,12},{12,11},... | collective-permute-start | bytes 1572872 | tf_op jit(solution)/shard_map/ppermute | solution.py:34

commit v3 on v2

--- a/solution.py
+++ b/solution.py
@@ -9,7 +9,8 @@
 
 HIGHEST = lax.Precision.HIGHEST
 EXTRA = 8
-FIRST = (0, 3)
+FIRST = (3, 0)
+ORDER = (3, 0, 1, 2)
 F32, BF16 = jnp.float32, jnp.bfloat16
 ANY = pl.BlockSpec(memory_space=pl.ANY)
 VMEM = pl.BlockSpec(memory_space=pltpu.VMEM)
@@ -99,27 +100,12 @@
 def split_faces(load):
     size, columns = load.shape[0] // 4, load.shape[1]
 
-    def kernel(load_ref, *refs):
-        outs, sems = refs[:4], refs[4]
+    def kernel(load_ref, *outs):
         faces, _ = slots()
-        copies = [
-            pltpu.make_async_copy(load_ref.at[rows_of(faces[s], size)], outs[s], sems.at[s])
-            for s in range(4)
-        ]
-        for copy in copies:
-            copy.start()
-        for copy in copies:
-            copy.wait()
-
-    return call(
-        kernel,
-        [load],
-        [ANY],
-        [shape(size, columns)] * 4,
-        [VMEM] * 4,
-        [pltpu.SemaphoreType.DMA((4,))],
-        0,
-    )
+        for s in range(4):
+            outs[s][...] = load_ref[rows_of(faces[s], size), :]
+
+    return call(kernel, [load], [VMEM], [shape(size, columns)] * 4, [VMEM] * 4, [], 0)
 
 
 def assembled_first(own, got, orders):
@@ -148,7 +134,7 @@
     return own_refs[s][...] + exact(order_ref[face], got_refs[s][...])
 
 
-def gather_primal(own, got, orders, basis, tail):
+def gather_primal(own, got, orders, basis, tail, keep):
     size, columns = own[0].shape
     prim = basis.shape[0]
     whole = (4 * size, columns)
@@ -162,7 +148,7 @@
         spread = lambda part: {s: part[i] for i, s in enumerate(last)}
         own_refs, got_refs = spread(refs[:count]), spread(refs[count : 2 * count])
         refs = refs[2 * count :]
-        order_ref, basis_ref, tail_ref, full_ref, half_ref, sent_ref = refs
+        order_ref, basis_ref, tail_ref, full_ref, sent_ref, half_ref = refs
         faces, weights = slots()
         sent_ref[prim:, :] = tail_ref[...]
         for s in range(4):
@@ -175,13 +161,10 @@
         kernel,
         [first, *own, *got, orders, basis, tail],
         [VMEM] * (4 + 2 * count),
-        [
-            shape(4, size, columns),
-            jax.ShapeDtypeStruct(whole, BF16),
-            shape(prim + tail.shape[0], columns),
-        ],
-        [VMEM] * 3,
-        [],
+        [shape(4, size, columns), shape(prim + tail.shape[0], columns)]
+        + [jax.ShapeDtypeStruct(whole, BF16)] * keep,
+        [VMEM] * (2 + keep),
+        [pltpu.VMEM(whole, BF16)] * (1 - keep),
         2 * 4 * size * columns * (2 * size + prim),
     )
 
@@ -402,7 +385,8 @@
     pieces = columns // sums.shape[2]
 
     def kernel(*refs):
-        own_refs, got_refs, order_ref = refs[:4], refs[4:8], refs[8]
+        own_refs, order_ref = refs[:4], refs[8]
+        got_refs = {s: refs[4 + k] for k, s in enumerate(ORDER)}
         search_ref, second_ref, residual_ref, image_ref, total_ref, sums_ref = refs[9:15]
         out_refs, (solution_buf, residual_buf, sems) = refs[15:17], refs[17:]
         faces, _ = slots()
@@ -427,7 +411,7 @@
 
     return call(
         kernel,
-        [*own, *got, orders, search, second, residual, image, total, sums],
+        [*own, *(got[s] for s in ORDER), orders, search, second, residual, image, total, sums],
         [VMEM] * 15,
         [shape(n, columns)] * 2,
         [ANY] * 2,
@@ -468,13 +452,13 @@
     index = primal_index.reshape(prim, 1)
     tail = level.tail(group_inverse[0], group_to_coarsest[0], primal_index)
 
-    residual, half, sent = gather_primal(own, got, orders, basis, tail)
+    residual, sent, half = gather_primal(own, got, orders, basis, tail, 1)
     gathered = lax.all_gather(sent, "cell", axis=0, tiled=False)
     sent, picked, up = lower_first(level, gathered, index, coarsest_inverse)
     ups = lax.all_gather(sent, "grp", axis=0, tiled=False)
     *own, picked = solve_first(half, local_inverse, lift, picked, up, ups)
     search, *own, sums = image_of(own, exchange(own), orders, schur, residual, (), 1)
-    image, _, sent = gather_primal(own, exchange(own), orders, basis, sums)
+    image, sent = gather_primal(own, exchange(own), orders, basis, sums, 0)
     again = lax.all_gather(sent, "cell", axis=0, tiled=False)
     sent = lower_second(level, gathered, index, ups, again)
     sent = lax.all_to_all(sent, "grp", 0, 0, tiled=True)

time: 171 us -> 170 us (level)
  starting transfers between devices: 32.6 us -> 27.1 us
  waiting for transfers between devices: 31.9 us -> 35.3 us
  blocking collectives: 74.7 us -> 76.6 us
    ppermute x20, starting transfers between devices: 32.6 us -> 27.1 us  [exchange(): got[slot] = lax.ppermute(parts[slot], axis, pairs(lax.axis_size(axis), odd))]
    ppermute x20, waiting for transfers between devices: 31.9 us -> 35.3 us  [exchange(): got[slot] = lax.ppermute(parts[slot], axis, pairs(lax.axis_size(axis), odd))]
where the time goes in v3:
time: 170 us; the launch traced here: 169 us
  blocking collectives  76.6 us (45%)
  waiting for transfers between devices  35.3 us (21%)
  starting transfers between devices  27.1 us (16%)
  Pallas kernels  26.4 us (16%)
  local copies, waits for them, and re-layouts  2.01 us (1%)
    ppermute x20, waiting for transfers between devices, exchange(): got[slot] = lax.ppermute(parts[slot], axis, pairs(lax.axis_size(axis), odd))  35.3 us
    ppermute x20, starting transfers between devices, exchange(): got[slot] = lax.ppermute(parts[slot], axis, pairs(lax.axis_size(axis), odd))  27.1 us
    pallas_call x14, Pallas kernels, call(): pl.pallas_call(kernel, out_shape=outs, in_specs=specs, out_specs=out_spec...  26.4 us
    all_gather x1, blocking collectives, body(): ups = lax.all_gather(sent, 'grp', axis=0, tiled=False)  19.4 us
    all_to_all x1, blocking collectives, body(): sums = lax.all_to_all(sums, ('grp', 'cell'), 0, 0, tiled=True)  17.5 us
    all_gather x1, blocking collectives, body(): gathered = lax.all_gather(sent, 'cell', axis=0, tiled=False)  14.9 us
    all_gather x1, blocking collectives, body(): again = lax.all_gather(sent, 'cell', axis=0, tiled=False)  13.1 us
    all_to_all x1, blocking collectives, body(): sent = lax.all_to_all(sent, 'grp', 0, 0, tiled=True)  11.7 us
  transfers between devices with their start and end apart: 20, of which 4 were waited for; matrix products, arithmetic and copies ran while one was open for 1% of the time, Pallas kernels for 2%

profile of v3, /device:TPU:0, one launch (start us, length us, event | category | flops | bytes accessed | tf_op | source)
XLA Modules:
  0.0 169.2 jit_solution(9804942365046729601)
XLA Ops:
  0.7 1.6 copy-done
  2.3 0.9 shard_map.104
  3.2 0.7 collective-permute-start
  3.9 3.1 %collective-permute-start.1 = (f32[512,256]{1,0:T(8,128)S(1)}, f32[512,256]{1,0:T(8,128)S(1)}, u32[]{:S(2)}, u32[]{:S(2)}) collective-permute-start(f32[512,256]{1,0:T(8,128)S(1)} %get-tuple-element.40.refs_1_), channel_id=1, source_target_pairs={{0,8},{8,0},{16,24},{24,16},{1,9},{9,1},{17,25},{25,17},{2,10},{10... | collective-permute-start | bytes 1572872 | tf_op jit(solution)/shard_map/ppermute | solution.py:35
  7.0 1.5 collective-permute-start.2
  8.4 2.5 %collective-permute-start.3 = (f32[512,256]{1,0:T(8,128)}, f32[512,256]{1,0:T(8,128)}, u32[]{:S(2)}, u32[]{:S(2)}) collective-permute-start(f32[512,256]{1,0:T(8,128)} %get-tuple-element.42.refs_1_), channel_id=1, source_target_pairs={{0,1},{1,0},{2,3},{3,2},{4,5},{5,4},{6,7},{7,6},{8,9},{9,8},{10,11... | collective-permute-start | bytes 1572872 | tf_op jit(solution)/shard_map/ppermute | solution.py:35
  11.0 0.1 copy.13.index_ref
  11.1 0.3 copy.11
  11.4 0.5 fusion.refs_4_.refs_8_
  11.9 5.5 %collective-permute-done.1.refs_3_ = f32[512,256]{1,0:T(8,128)S(1)} collective-permute-done((f32[512,256]{1,0:T(8,128)S(1)}, f32[512,256]{1,0:T(8,128)S(1)}, u32[]{:S(2)}, u32[]{:S(2)}) %collective-permute-start.1) | collective-permute-done | bytes 524320 | tf_op jit(solution)/shard_map/ppermute | solution.py:35
  17.4 0.7 shard_map.105.first_ref
  18.2 0.0 slice-start.1
  18.2 2.8 %shard_map.106 = (f32[4,512,256]{2,1,0:T(8,128)S(1)}, f32[88,256]{1,0:T(8,128)S(1)}, bf16[2048,256]{1,0:T(8,128)(2,1)S(1)}) custom-call(f32[2,512,256]{2,1,0:T(8,128)S(1)} %shard_map.105.first_ref, f32[512,256]{1,0:T(8,128)S(1)} %get-tuple-element.41.refs_0_, f32[512,256]{1,0:T(8,128)} %get-tuple-element.42.refs_1_, ...), custom_call_target="tpu_custom_call" | custom-call | flops 1107296256 | bytes 678912 | tf_op jit(solution)/shard_map/pallas_call | solution.py:85
  21.0 14.9 %all-gather = f32[704,256]{1,0:T(8,128)S(1)} all-gather(f32[88,256]{1,0:T(8,128)S(1)} %get-tuple-element.45), channel_id=2, replica_groups=mesh['grp'=4,'cell'=8] {'cell'}, dimensions={0}, use_global_device_ids=true | all-gather | bytes 811008 | tf_op jit(solution)/shard_map/all_gather | solution.py:456
  35.9 1.1 shard_map.107
  37.0 19.4 %all-gather.1 = f32[576,256]{1,0:T(8,128)S(1)} all-gather(f32[144,256]{1,0:T(8,128)S(1)} %get-tuple-element.48), channel_id=3, replica_groups=mesh['grp'=4,'cell'=8] {'grp'}, dimensions={0}, use_global_device_ids=true | all-gather | bytes 737280 | tf_op jit(solution)/shard_map/all_gather | solution.py:458
  56.5 3.1 %shard_map.108 = (f32[512,256]{1,0:T(8,128)S(1)}, f32[512,256]{1,0:T(8,128)S(1)}, f32[512,256]{1,0:T(8,128)S(1)}, f32[512,256]{1,0:T(8,128)S(1)}, f32[32,256]{1,0:T(8,128)S(1)}) custom-call(bf16[2048,256]{1,0:T(8,128)(2,1)S(1)} %get-tuple-element.44.half_ref, bf16[2048,2048]{1,0:T(8,128)(2,1)S(1)} %bitcast.21, bf16[2048,32]{1,0:T(8,128)(2,1)S(1)} %bitcast.31, ...), custom_call_target="tpu_custom_call" | custom-call | flops 2147483648 | bytes 1275904 | tf_op jit(solution)/shard_map/pallas_call | solution.py:85
  59.6 0.7 collective-permute-start.4
  60.3 0.1 collective-permute-start.5
  60.4 0.7 collective-permute-start.6
  61.1 1.8 %collective-permute-start.7 = (f32[512,256]{1,0:T(8,128)S(1)}, f32[512,256]{1,0:T(8,128)S(1)}, u32[]{:S(2)}, u32[]{:S(2)}) collective-permute-start(f32[512,256]{1,0:T(8,128)S(1)} %get-tuple-element.52.refs_1_), channel_id=1, source_target_pairs={{0,1},{1,0},{2,3},{3,2},{4,5},{5,4},{6,7},{7,6},{8,9},{9,8},{10,11... | collective-permute-start | bytes 1572872 | tf_op jit(solution)/shard_map/ppermute | solution.py:35
  62.9 11.5 %collective-permute-done.5.refs_3_ = f32[512,256]{1,0:T(8,128)S(1)} collective-permute-done((f32[512,256]{1,0:T(8,128)S(1)}, f32[512,256]{1,0:T(8,128)S(1)}, u32[]{:S(2)}, u32[]{:S(2)}) %collective-permute-start.5) | collective-permute-done | bytes 524320 | tf_op jit(solution)/shard_map/ppermute | solution.py:35
  74.4 0.7 shard_map.109.first_ref
  75.2 3.1 %shard_map.110 = (f32[4,512,256]{2,1,0:T(8,128)S(1)}, f32[512,256]{1,0:T(8,128)S(1)}, f32[512,256]{1,0:T(8,128)S(1)}, f32[512,256]{1,0:T(8,128)S(1)}, f32[512,256]{1,0:T(8,128)S(1)}, /*index=5*/f32[8,256]{1,0:T(8,128)S(1)}) custom-call(f32[2,512,256]{2,1,0:T(8,128)S(1)} %shard_map.109.first_ref, f32[512,256]{1,0:T(8,128)S(1)} %get-tuple-element.51.refs_0_, ...), custom_call_target="tpu_custom_call" | custom-call | flops 3221225472 | bytes 1966080 | tf_op jit(solution)/shard_map/pallas_call | solution.py:85
  78.3 0.7 collective-permute-start.8
  79.0 3.5 %collective-permute-start.9 = (f32[512,256]{1,0:T(8,128)S(1)}, f32[512,256]{1,0:T(8,128)S(1)}, u32[]{:S(2)}, u32[]{:S(2)}) collective-permute-start(f32[512,256]{1,0:T(8,128)S(1)} %get-tuple-element.54.refs_1_.refs_7_), channel_id=1, source_target_pairs={{0,8},{8,0},{16,24},{24,16},{1,9},{9,1},{17,25},{25,17},{2,10},{10... | collective-permute-start | bytes 1572872 | tf_op jit(solution)/shard_map/ppermute | solution.py:35
  82.5 0.7 collective-permute-start.10
  83.2 2.9 %collective-permute-start.11 = (f32[512,256]{1,0:T(8,128)S(1)}, f32[512,256]{1,0:T(8,128)S(1)}, u32[]{:S(2)}, u32[]{:S(2)}) collective-permute-start(f32[512,256]{1,0:T(8,128)S(1)} %get-tuple-element.56.refs_1_.refs_9_), channel_id=1, source_target_pairs={{0,1},{1,0},{2,3},{3,2},{4,5},{5,4},{6,7},{7,6},{8,9},{9,8},{10,11... | collective-permute-start | bytes 1572872 | tf_op jit(solution)/shard_map/ppermute | solution.py:35
  86.2 6.6 %collective-permute-done.9.refs_3_ = f32[512,256]{1,0:T(8,128)S(1)} collective-permute-done((f32[512,256]{1,0:T(8,128)S(1)}, f32[512,256]{1,0:T(8,128)S(1)}, u32[]{:S(2)}, u32[]{:S(2)}) %collective-permute-start.9) | collective-permute-done | bytes 524320 | tf_op jit(solution)/shard_map/ppermute | solution.py:35
  92.8 0.7 shard_map.111.first_ref
  93.6 1.3 shard_map.112
  94.9 13.1 %all-gather.2 = f32[320,256]{1,0:T(8,128)S(1)} all-gather(f32[40,256]{1,0:T(8,128)S(1)} %get-tuple-element.60), channel_id=4, replica_groups=mesh['grp'=4,'cell'=8] {'cell'}, dimensions={0}, use_global_device_ids=true | all-gather | bytes 368640 | tf_op jit(solution)/shard_map/all_gather | solution.py:462
  108.0 1.4 shard_map.113
  109.4 11.7 %all_to_all.10.sent_ref = f32[4,40,256]{2,1,0:T(8,128)S(1)} all-to-all(f32[4,40,256]{2,1,0:T(8,128)S(1)} %shard_map.113), channel_id=1, replica_groups=mesh['grp'=4,'cell'=8] {'grp'}, dimensions={0} | all-to-all | bytes 327680 | tf_op jit(solution)/shard_map/all_to_all | solution.py:464
  121.0 2.9 %shard_map.114 = (f32[512,256]{1,0:T(8,128)S(1)}, f32[512,256]{1,0:T(8,128)S(1)}, f32[512,256]{1,0:T(8,128)S(1)}, f32[512,256]{1,0:T(8,128)S(1)}, f32[4,512,256]{2,1,0:T(8,128)S(1)}, /*index=5*/f32[8,256]{1,0:T(8,128)S(1)}) custom-call(f32[4,512,256]{2,1,0:T(8,128)S(1)} %get-tuple-element.43.refs_6_.residual_ref, ...), custom_call_target="tpu_custom_call" | custom-call | flops 2147483648 | bytes 1613824 | tf_op jit(solution)/shard_map/pallas_call | solution.py:85
  124.0 0.7 collective-permute-start.12
  124.7 0.7 collective-permute-start.13
  125.4 0.7 collective-permute-start.14
  126.1 1.3 collective-permute-start.15
  127.4 11.7 %collective-permute-done.13.refs_3_ = f32[512,256]{1,0:T(8,128)S(1)} collective-permute-done((f32[512,256]{1,0:T(8,128)S(1)}, f32[512,256]{1,0:T(8,128)S(1)}, u32[]{:S(2)}, u32[]{:S(2)}) %collective-permute-start.13) | collective-permute-done | bytes 524320 | tf_op jit(solution)/shard_map/ppermute | solution.py:35
  139.1 0.8 shard_map.115.first_ref
  139.8 3.2 %shard_map.116 = (f32[4,512,256]{2,1,0:T(8,128)S(1)}, f32[512,256]{1,0:T(8,128)S(1)}, f32[512,256]{1,0:T(8,128)S(1)}, f32[512,256]{1,0:T(8,128)S(1)}, f32[512,256]{1,0:T(8,128)S(1)}, /*index=5*/f32[8,128]{1,0:T(8,128)S(1)}) custom-call(f32[2,512,256]{2,1,0:T(8,128)S(1)} %shard_map.115.first_ref, f32[512,256]{1,0:T(8,128)S(1)} %get-tuple-element.63.refs_0_, ...), custom_call_target="tpu_custom_call" | custom-call | flops 3221225472 | bytes 2228224 | tf_op jit(solution)/shard_map/pallas_call | solution.py:85
  143.1 3.4 %collective-permute-start.17 = (f32[512,256]{1,0:T(8,128)S(1)}, f32[512,256]{1,0:T(8,128)S(1)}, u32[]{:S(2)}, u32[]{:S(2)}) collective-permute-start(f32[512,256]{1,0:T(8,128)S(1)} %get-tuple-element.66.refs_0_), channel_id=1, source_target_pairs={{0,8},{8,0},{16,24},{24,16},{1,9},{9,1},{17,25},{25,17},{2,10},{10... | collective-permute-start | bytes 1572872 | tf_op jit(solution)/shard_map/ppermute | solution.py:35
  146.5 0.7 collective-permute-start.18
  147.2 0.1 collective-permute-start.19
  147.3 0.7 collective-permute-start.16
  148.0 17.5 %all_to_all.11.refs_14_ = f32[32,8,128]{2,1,0:T(8,128)S(1)} all-to-all(f32[32,8,128]{2,1,0:T(8,128)S(1)} %broadcast_in_dim.6), channel_id=1, replica_groups=mesh['grp'=4,'cell'=8] {'grp','cell'}, dimensions={0} | all-to-all | bytes 262144 | tf_op jit(solution)/shard_map/all_to_all | solution.py:471
  165.5 3.5 %shard_map.117 = (f32[2048,256]{1,0:T(8,128)}, f32[2048,256]{1,0:T(8,128)}) custom-call(f32[512,256]{1,0:T(8,128)S(1)} %get-tuple-element.66.refs_0_, f32[512,256]{1,0:T(8,128)S(1)} %get-tuple-element.67.refs_1_, f32[512,256]{1,0:T(8,128)S(1)} %get-tuple-element.68.refs_2_, f32[512,256]{1,0:T(8,128)S(1)} %get-tuple-element.69.refs_3_, ...), custom_call_target="tpu_custom_call" | custom-call | flops 1073741824 | bytes 1852416 | tf_op jit(solution)/shard_map/pallas_call | solution.py:85
  (42 shorter events, 0.1 us)
Async XLA Ops:
  0.6 10.3 %copy-start.6 = (s32[1,32]{1,0:T(1,128)S(1)}, s32[1,32]{1,0:T(1,128)}, u32[]{:S(2)}) copy-start(s32[1,32]{1,0:T(1,128)} %param.14) | copy-start | bytes 388
  0.6 1.6 copy-start
  2.2 8.7 %copy-start.4 = (f32[1,32,128]{2,1,0:T(8,128)S(1)}, f32[1,32,128]{2,1,0:T(8,128)}, u32[]{:S(2)}) copy-start(f32[1,32,128]{2,1,0:T(8,128)} %param.16) | copy-start | bytes 49156
  2.2 8.8 %copy-start.1 = (bf16[1,32,2048]{2,1,0:T(8,128)(2,1)S(1)}, bf16[1,32,2048]{2,1,0:T(8,128)(2,1)}, u32[]{:S(2)}) copy-start(bf16[1,32,2048]{2,1,0:T(8,128)(2,1)} %param.13) | copy-start | bytes 393220
  2.2 9.1 %copy-start.3 = (f32[1,32,256]{2,1,0:T(8,128)S(1)}, f32[1,32,256]{2,1,0:T(8,128)}, u32[]{:S(2)}) copy-start(f32[1,32,256]{2,1,0:T(8,128)} %param.15) | copy-start | bytes 98308
  2.2 9.1 %copy-start.5 = (s32[1,4,512]{2,1,0:T(4,128)S(1)}, s32[1,4,512]{2,1,0:T(4,128)}, u32[]{:S(2)}) copy-start(s32[1,4,512]{2,1,0:T(4,128)} %param.12) | copy-start | bytes 24580
  3.2 8.7 %collective-permute-start = (f32[512,256]{1,0:T(8,128)S(1)}, f32[512,256]{1,0:T(8,128)S(1)}, u32[]{:S(2)}, u32[]{:S(2)}) collective-permute-start(f32[512,256]{1,0:T(8,128)S(1)} %get-tuple-element.39.refs_0_), channel_id=1, source_target_pairs={{1,2},{2,1},{3,4},{4,3},{5,6},{6,5},{9,10},{10,9},{11,12},{12,11},... | collective-permute-start | bytes 1572872 | tf_op jit(solution)/shard_map/ppermute | solution.py:35
  3.9 13.5 %collective-permute-start.1 = (f32[512,256]{1,0:T(8,128)S(1)}, f32[512,256]{1,0:T(8,128)S(1)}, u32[]{:S(2)}, u32[]{:S(2)}) collective-permute-start(f32[512,256]{1,0:T(8,128)S(1)} %get-tuple-element.40.refs_1_), channel_id=1, source_target_pairs={{0,8},{8,0},{16,24},{24,16},{1,9},{9,1},{17,25},{25,17},{2,10},{10... | collective-permute-start | bytes 1572872 | tf_op jit(solution)/shard_map/ppermute | solution.py:35
  7.0 11.2 %collective-permute-start.2 = (f32[512,256]{1,0:T(8,128)S(1)}, f32[512,256]{1,0:T(8,128)}, u32[]{:S(2)}, u32[]{:S(2)}) collective-permute-start(f32[512,256]{1,0:T(8,128)S(1)} %get-tuple-element.41.refs_0_), channel_id=1, source_target_pairs={{8,16},{16,8},{9,17},{17,9},{10,18},{18,10},{11,19},{19,11},{12,20... | collective-permute-start | bytes 1572872 | tf_op jit(solution)/shard_map/ppermute | solution.py:35
  8.4 9.7 %collective-permute-start.3 = (f32[512,256]{1,0:T(8,128)}, f32[512,256]{1,0:T(8,128)}, u32[]{:S(2)}, u32[]{:S(2)}) collective-permute-start(f32[512,256]{1,0:T(8,128)} %get-tuple-element.42.refs_1_), channel_id=1, source_target_pairs={{0,1},{1,0},{2,3},{3,2},{4,5},{5,4},{6,7},{7,6},{8,9},{9,8},{10,11... | collective-permute-start | bytes 1572872 | tf_op jit(solution)/shard_map/ppermute | solution.py:35
  11.4 45.1 %slice-start = ((s8[8388608]{0:T(1024)(128)(4,1)}), s8[4194304]{0:T(1024)(128)(4,1)S(1)}, s32[]{:S(2)}) async-start(s8[8388608]{0:T(1024)(128)(4,1)} %bitcast.19), calls=%async_computation.2 | async-start | bytes 8388608
  18.2 17.7 %copy-start.2 = (f32[128,128]{1,0:T(8,128)S(1)}, f32[128,128]{1,0:T(8,128)}, u32[]{:S(2)}) copy-start(f32[128,128]{1,0:T(8,128)} %coarsest_ref.1) | copy-start | bytes 196612
  18.2 38.3 %slice-start.1 = ((s8[8388608]{0:T(1024)(128)(4,1)}), s8[4194304]{0:T(1024)(128)(4,1)S(1)}, s32[]{:S(2)}) async-start(s8[8388608]{0:T(1024)(128)(4,1)} %bitcast.19), calls=%async_computation.3 | async-start | bytes 8388608
  37.0 38.1 %slice-start.2 = ((s8[8388608]{0:T(1024)(128)(4,1)}), s8[4194304]{0:T(1024)(128)(4,1)S(1)}, s32[]{:S(2)}) async-start(s8[8388608]{0:T(1024)(128)(4,1)} %bitcast.23), calls=%async_computation.4 | async-start | bytes 8388608
  56.5 18.7 %slice-start.3 = ((s8[8388608]{0:T(1024)(128)(4,1)}), s8[4194304]{0:T(1024)(128)(4,1)S(1)}, s32[]{:S(2)}) async-start(s8[8388608]{0:T(1024)(128)(4,1)} %bitcast.23), calls=%async_computation.5 | async-start | bytes 8388608
  59.6 3.3 %collective-permute-start.4 = (f32[512,256]{1,0:T(8,128)S(1)}, f32[512,256]{1,0:T(8,128)S(1)}, u32[]{:S(2)}, u32[]{:S(2)}) collective-permute-start(f32[512,256]{1,0:T(8,128)S(1)} %get-tuple-element.49.refs_0_), channel_id=1, source_target_pairs={{1,2},{2,1},{3,4},{4,3},{5,6},{6,5},{9,10},{10,9},{11,12},{12,11},... | collective-permute-start | bytes 1572872 | tf_op jit(solution)/shard_map/ppermute | solution.py:35
  60.3 14.1 %collective-permute-start.5 = (f32[512,256]{1,0:T(8,128)S(1)}, f32[512,256]{1,0:T(8,128)S(1)}, u32[]{:S(2)}, u32[]{:S(2)}) collective-permute-start(f32[512,256]{1,0:T(8,128)S(1)} %get-tuple-element.50.refs_1_), channel_id=1, source_target_pairs={{0,8},{8,0},{16,24},{24,16},{1,9},{9,1},{17,25},{25,17},{2,10},{10... | collective-permute-start | bytes 1572872 | tf_op jit(solution)/shard_map/ppermute | solution.py:35
  60.4 14.8 %collective-permute-start.6 = (f32[512,256]{1,0:T(8,128)S(1)}, f32[512,256]{1,0:T(8,128)S(1)}, u32[]{:S(2)}, u32[]{:S(2)}) collective-permute-start(f32[512,256]{1,0:T(8,128)S(1)} %get-tuple-element.51.refs_0_), channel_id=1, source_target_pairs={{8,16},{16,8},{9,17},{17,9},{10,18},{18,10},{11,19},{19,11},{12,20... | collective-permute-start | bytes 1572872 | tf_op jit(solution)/shard_map/ppermute | solution.py:35
  61.1 14.1 %collective-permute-start.7 = (f32[512,256]{1,0:T(8,128)S(1)}, f32[512,256]{1,0:T(8,128)S(1)}, u32[]{:S(2)}, u32[]{:S(2)}) collective-permute-start(f32[512,256]{1,0:T(8,128)S(1)} %get-tuple-element.52.refs_1_), channel_id=1, source_target_pairs={{0,1},{1,0},{2,3},{3,2},{4,5},{5,4},{6,7},{7,6},{8,9},{9,8},{10,11... | collective-permute-start | bytes 1572872 | tf_op jit(solution)/shard_map/ppermute | solution.py:35
  78.3 7.8 %collective-permute-start.8 = (f32[512,256]{1,0:T(8,128)S(1)}, f32[512,256]{1,0:T(8,128)S(1)}, u32[]{:S(2)}, u32[]{:S(2)}) collective-permute-start(f32[512,256]{1,0:T(8,128)S(1)} %get-tuple-element.53.refs_0_.refs_10_), channel_id=1, source_target_pairs={{1,2},{2,1},{3,4},{4,3},{5,6},{6,5},{9,10},{10,9},{11,12},{12,11},... | collective-permute-start | bytes 1572872 | tf_op jit(solution)/shard_map/ppermute | solution.py:35
  79.0 13.8 %collective-permute-start.9 = (f32[512,256]{1,0:T(8,128)S(1)}, f32[512,256]{1,0:T(8,128)S(1)}, u32[]{:S(2)}, u32[]{:S(2)}) collective-permute-start(f32[512,256]{1,0:T(8,128)S(1)} %get-tuple-element.54.refs_1_.refs_7_), channel_id=1, source_target_pairs={{0,8},{8,0},{16,24},{24,16},{1,9},{9,1},{17,25},{25,17},{2,10},{10... | collective-permute-start | bytes 1572872 | tf_op jit(solution)/shard_map/ppermute | solution.py:35
  82.5 11.0 %collective-permute-start.10 = (f32[512,256]{1,0:T(8,128)S(1)}, f32[512,256]{1,0:T(8,128)S(1)}, u32[]{:S(2)}, u32[]{:S(2)}) collective-permute-start(f32[512,256]{1,0:T(8,128)S(1)} %get-tuple-element.55.refs_0_.refs_8_), channel_id=1, source_target_pairs={{8,16},{16,8},{9,17},{17,9},{10,18},{18,10},{11,19},{19,11},{12,20... | collective-permute-start | bytes 1572872 | tf_op jit(solution)/shard_map/ppermute | solution.py:35
  83.2 10.3 %collective-permute-start.11 = (f32[512,256]{1,0:T(8,128)S(1)}, f32[512,256]{1,0:T(8,128)S(1)}, u32[]{:S(2)}, u32[]{:S(2)}) collective-permute-start(f32[512,256]{1,0:T(8,128)S(1)} %get-tuple-element.56.refs_1_.refs_9_), channel_id=1, source_target_pairs={{0,1},{1,0},{2,3},{3,2},{4,5},{5,4},{6,7},{7,6},{8,9},{9,8},{10,11... | collective-permute-start | bytes 1572872 | tf_op jit(solution)/shard_map/ppermute | solution.py:35
  124.0 3.4 %collective-permute-start.12 = (f32[512,256]{1,0:T(8,128)S(1)}, f32[512,256]{1,0:T(8,128)S(1)}, u32[]{:S(2)}, u32[]{:S(2)}) collective-permute-start(f32[512,256]{1,0:T(8,128)S(1)} %get-tuple-element.61.refs_0_), channel_id=1, source_target_pairs={{1,2},{2,1},{3,4},{4,3},{5,6},{6,5},{9,10},{10,9},{11,12},{12,11},... | collective-permute-start | bytes 1572872 | tf_op jit(solution)/shard_map/ppermute | solution.py:35
  124.7 14.4 %collective-permute-start.13 = (f32[512,256]{1,0:T(8,128)S(1)}, f32[512,256]{1,0:T(8,128)S(1)}, u32[]{:S(2)}, u32[]{:S(2)}) collective-permute-start(f32[512,256]{1,0:T(8,128)S(1)} %get-tuple-element.62.refs_1_), channel_id=1, source_target_pairs={{0,8},{8,0},{16,24},{24,16},{1,9},{9,1},{17,25},{25,17},{2,10},{10... | collective-permute-start | bytes 1572872 | tf_op jit(solution)/shard_map/ppermute | solution.py:35
  125.4 14.4 %collective-permute-start.14 = (f32[512,256]{1,0:T(8,128)S(1)}, f32[512,256]{1,0:T(8,128)S(1)}, u32[]{:S(2)}, u32[]{:S(2)}) collective-permute-start(f32[512,256]{1,0:T(8,128)S(1)} %get-tuple-element.63.refs_0_), channel_id=1, source_target_pairs={{8,16},{16,8},{9,17},{17,9},{10,18},{18,10},{11,19},{19,11},{12,20... | collective-permute-start | bytes 1572872 | tf_op jit(solution)/shard_map/ppermute | solution.py:35
  126.1 13.7 %collective-permute-start.15 = (f32[512,256]{1,0:T(8,128)S(1)}, f32[512,256]{1,0:T(8,128)S(1)}, u32[]{:S(2)}, u32[]{:S(2)}) collective-permute-start(f32[512,256]{1,0:T(8,128)S(1)} %get-tuple-element.64.refs_1_), channel_id=1, source_target_pairs={{0,1},{1,0},{2,3},{3,2},{4,5},{5,4},{6,7},{7,6},{8,9},{9,8},{10,11... | collective-permute-start | bytes 1572872 | tf_op jit(solution)/shard_map/ppermute | solution.py:35
  143.1 22.3 %collective-permute-start.17 = (f32[512,256]{1,0:T(8,128)S(1)}, f32[512,256]{1,0:T(8,128)S(1)}, u32[]{:S(2)}, u32[]{:S(2)}) collective-permute-start(f32[512,256]{1,0:T(8,128)S(1)} %get-tuple-element.66.refs_0_), channel_id=1, source_target_pairs={{0,8},{8,0},{16,24},{24,16},{1,9},{9,1},{17,25},{25,17},{2,10},{10... | collective-permute-start | bytes 1572872 | tf_op jit(solution)/shard_map/ppermute | solution.py:35
  146.5 18.9 %collective-permute-start.18 = (f32[512,256]{1,0:T(8,128)S(1)}, f32[512,256]{1,0:T(8,128)S(1)}, u32[]{:S(2)}, u32[]{:S(2)}) collective-permute-start(f32[512,256]{1,0:T(8,128)S(1)} %get-tuple-element.67.refs_1_), channel_id=1, source_target_pairs={{8,16},{16,8},{9,17},{17,9},{10,18},{18,10},{11,19},{19,11},{12,20... | collective-permute-start | bytes 1572872 | tf_op jit(solution)/shard_map/ppermute | solution.py:35
  147.2 18.3 %collective-permute-start.19 = (f32[512,256]{1,0:T(8,128)S(1)}, f32[512,256]{1,0:T(8,128)S(1)}, u32[]{:S(2)}, u32[]{:S(2)}) collective-permute-start(f32[512,256]{1,0:T(8,128)S(1)} %get-tuple-element.68.refs_2_), channel_id=1, source_target_pairs={{0,1},{1,0},{2,3},{3,2},{4,5},{5,4},{6,7},{7,6},{8,9},{9,8},{10,11... | collective-permute-start | bytes 1572872 | tf_op jit(solution)/shard_map/ppermute | solution.py:35
  147.3 18.2 %collective-permute-start.16 = (f32[512,256]{1,0:T(8,128)S(1)}, f32[512,256]{1,0:T(8,128)S(1)}, u32[]{:S(2)}, u32[]{:S(2)}) collective-permute-start(f32[512,256]{1,0:T(8,128)S(1)} %get-tuple-element.69.refs_3_), channel_id=1, source_target_pairs={{1,2},{2,1},{3,4},{4,3},{5,6},{6,5},{9,10},{10,9},{11,12},{12,11},... | collective-permute-start | bytes 1572872 | tf_op jit(solution)/shard_map/ppermute | solution.py:35
